TPU v7x, 32 devices: a whole 2x2x4 slice. The times are simulated.
32 devices in a mesh: dp: 8 (over y, x, core), tensor: 4 (over z).
Axes of the slice: x: 2, y: 2, z: 4, core: 2. Of those that a mesh axis runs over, the one named last changes fastest.
Arguments:
- inputs: bfloat16 [8192, 2048], P('dp'), may hold values from -6 to 6
- cotangent: bfloat16 [8192, 2048], P('dp'), may hold values from -6 to 6
- segments: int32 [8, 1024], P('dp'), may hold values from 0 to 3, never falling along the last dimension, each value on 1 to 512 neighbouring positions
- subsets: int32 [8], P('dp'), may hold values from 0 to 21
- ln1_gain: float32 [2048], replicated, may hold values from 0.5 to 1.5
- ln1_bias: float32 [2048], replicated, may hold values from -2 to 2
- qkv_weight: bfloat16 [2048, 6144], P(None, 'tensor'), may hold values from -0.125 to 0.125
- qkv_bias: float32 [6144], P('tensor'), may hold values from -2 to 2
- dense_weight: bfloat16 [2048, 2048], P('tensor'), may hold values from -0.5 to 0.5
- dense_bias: float32 [2048], replicated, may hold values from -3 to 3
- ln2_gain: float32 [2048], replicated, may hold values from 0.5 to 1.5
- ln2_bias: float32 [2048], replicated, may hold values from -2 to 2
- up_weight: bfloat16 [2048, 8192], P(None, 'tensor'), may hold values from -0.125 to 0.125
- up_bias: float32 [8192], P('tensor'), may hold values from -3 to 3
- down_weight: bfloat16 [8192, 2048], P('tensor'), may hold values from -0.0625 to 0.0625
- down_bias: float32 [2048], replicated, may hold values from -3 to 3
Outputs:
- out: bfloat16 [8192, 2048], P('dp')
- input_grad: bfloat16 [8192, 2048], P('dp')
- ln1_gain_grad: float32 [2048], replicated
- ln1_bias_grad: float32 [2048], replicated
- qkv_weight_grad: float32 [2048, 6144], P('dp', 'tensor')
- qkv_bias_grad: float32 [6144], P('tensor')
- dense_weight_grad: float32 [2048, 2048], P('tensor', 'dp')
- dense_bias_grad: float32 [2048], replicated
- ln2_gain_grad: float32 [2048], replicated
- ln2_bias_grad: float32 [2048], replicated
- up_weight_grad: float32 [2048, 8192], P('dp', 'tensor')
- up_bias_grad: float32 [8192], P('tensor')
- down_weight_grad: float32 [8192, 2048], P('tensor', 'dp')
- down_bias_grad: float32 [2048], replicated
- subset_rms: float32 [22, 2], replicated
Inputs may be any that keep to these rules, and one draw needn't show every extreme that they name: `segments`: within each sequence the document numbers never fall; every document has 1 to 512 tokens and one has exactly 512.
All inputs are finite; a program needn't handle non-finite values.
Results may differ from a plain program's by a relative error of at most 0.0094.
Values sent between devices are 32-bit elements; how exact they have to be, the bound alone decides.
A program may use at most 256 MiB of HBM per device.

v0:
```python
import jax
import jax.numpy as jnp
from jax import lax
from jax.sharding import PartitionSpec as P

HEADS = 8
HS = 256
ROT = 64
FF = 8192
SUBSETS = 22
LEN = 1024


EPSILON = 1e-05
MASKED_SCORE = -1000000000.0


def layer_norm(resid, norm_gain, norm_bias):
    centre = resid - jnp.mean(resid, axis=-1, keepdims=True)
    variance = jnp.mean(centre * centre, axis=-1, keepdims=True)
    return centre * lax.rsqrt(variance + EPSILON) * norm_gain + norm_bias


def rotary_tables(length):
    half_rot = ROT // 2
    frequency = 10000.0 ** (-(2.0 * jnp.arange(half_rot, dtype=jnp.float32)) / ROT)
    angles = jnp.arange(length, dtype=jnp.float32)[:, None] * frequency[None, :]
    angles = jnp.concatenate([angles, angles], axis=1)
    return (jnp.cos(angles), jnp.sin(angles))


def rotate(heads_in, cosine, sine_table):
    rot_part = heads_in[..., :ROT]
    turned = jnp.concatenate([-rot_part[..., ROT // 2 :], rot_part[..., : ROT // 2]], axis=-1)
    rot_part = rot_part * cosine[:, None, :] + turned * sine_table[:, None, :]
    return jnp.concatenate([rot_part, heads_in[..., ROT:]], axis=-1)


def gelu_exact(hidden):
    return jax.nn.gelu(hidden, approximate=False)


def dot_rows(left, right):
    return lax.dot_general(
        left, right, (((0,), (0,)), ((), ())), preferred_element_type=jnp.float32
    )


def dot_cols(left, right):
    return lax.dot_general(
        left, right, (((1,), (1,)), ((), ())), preferred_element_type=jnp.float32
    )


def masked_scores(query_block, key_rows, segment_row, row_start, score_scale):
    scores = (
        jnp.einsum("qhd,khd->hqk", query_block, key_rows, preferred_element_type=jnp.float32)
        * score_scale
    )
    query_places = row_start + jnp.arange(query_block.shape[0])
    key_places = jnp.arange(key_rows.shape[0])
    query_segs = lax.dynamic_slice_in_dim(segment_row, row_start, query_block.shape[0], 0)
    allowed = (query_segs[:, None] == segment_row[None, :]) & (
        key_places[None, :] <= query_places[:, None]
    )
    return jnp.where(allowed[None], scores, MASKED_SCORE)


def on_device(
    inputs,
    cotangent,
    segments,
    subsets,
    ln1_gain,
    ln1_bias,
    qkv_weight,
    qkv_bias,
    dense_weight,
    dense_bias,
    ln2_gain,
    ln2_bias,
    up_weight,
    up_bias,
    down_weight,
    down_bias,
):
    rows_here = inputs.shape[0]
    seqs_here = segments.shape[0]
    heads_here = dense_weight.shape[0] // HS
    block_rows = min(512, LEN)
    score_scale = HS ** (-0.5)
    resid = inputs.astype(jnp.float32)
    first_full, pull_first = jax.vjp(layer_norm, resid, ln1_gain, ln1_bias)
    first_norm = first_full.astype(jnp.bfloat16)
    joined = jnp.dot(first_norm, qkv_weight, preferred_element_type=jnp.float32) + qkv_bias
    joined = joined.reshape(seqs_here, LEN, heads_here, 3, HS)
    cosine, sine_table = rotary_tables(LEN)

    def turn(heads_in):
        return rotate(heads_in, cosine, sine_table)

    query_full, pull_turn = jax.vjp(turn, joined[:, :, :, 0])
    queries = query_full.astype(jnp.bfloat16)
    key_rows = turn(joined[:, :, :, 1]).astype(jnp.bfloat16)
    values = joined[:, :, :, 2].astype(jnp.bfloat16)

    def attend(seq_item):
        query_seq, key_seq, value_seq, segment_row = seq_item
        out_blocks = []
        total_blocks = []
        for row_start in range(0, LEN, block_rows):
            query_block = query_seq[row_start : row_start + block_rows]
            scores = masked_scores(query_block, key_seq, segment_row, row_start, score_scale)
            score_peak = jnp.max(scores, axis=-1, keepdims=True)
            weights = jnp.exp(scores - score_peak)
            weight_total = jnp.sum(weights, axis=-1, keepdims=True)
            attn_probs = (weights / weight_total).astype(jnp.bfloat16)
            out_blocks.append(
                jnp.einsum(
                    "hqk,khd->qhd", attn_probs, value_seq, preferred_element_type=jnp.float32
                )
            )
            total_blocks.append(score_peak + jnp.log(weight_total))
        return (jnp.concatenate(out_blocks, axis=0), jnp.concatenate(total_blocks, axis=1))

    context, log_totals = lax.map(attend, (queries, key_rows, values, segments))
    context_low = context.reshape(rows_here, heads_here * HS).astype(jnp.bfloat16)
    attn_part = jnp.dot(context_low, dense_weight, preferred_element_type=jnp.float32)
    second_full, pull_second = jax.vjp(layer_norm, resid, ln2_gain, ln2_bias)
    second_norm = second_full.astype(jnp.bfloat16)
    hidden = jnp.dot(second_norm, up_weight, preferred_element_type=jnp.float32) + up_bias
    active, pull_active = jax.vjp(gelu_exact, hidden)
    active_low = active.astype(jnp.bfloat16)
    branch_terms = attn_part + jnp.dot(active_low, down_weight, preferred_element_type=jnp.float32)
    branches = lax.psum(branch_terms, "tensor")
    out = (resid + branches + dense_bias + down_bias).astype(jnp.bfloat16)
    context_seq = jnp.sum((context * context).reshape(seqs_here, -1), axis=1)
    active_seq = jnp.sum((active * active).reshape(seqs_here, -1), axis=1)
    count_seq = jnp.where(lax.axis_index("tensor") == 0, float(LEN), 0.0) * jnp.ones_like(
        context_seq
    )
    subset_pick = (subsets[:, None] == jnp.arange(SUBSETS)[None, :]).astype(jnp.float32)
    per_seq = jnp.stack([context_seq, active_seq, count_seq], axis=1)
    stats_local = jnp.sum(subset_pick[:, :, None] * per_seq[:, None, :], axis=0)
    stats_total = lax.psum(stats_local, ("dp", "tensor"))
    grad_full = cotangent.astype(jnp.float32)
    out_bias_grad = jnp.sum(grad_full, axis=0)
    down_grad = dot_rows(active_low, cotangent)
    dense_grad = dot_rows(context_low, cotangent)
    d_active = dot_cols(cotangent, down_weight)
    d_hidden = pull_active(d_active)[0].astype(jnp.bfloat16)
    up_bias_grad = jnp.sum(d_hidden, axis=0, dtype=jnp.float32)
    d_second = dot_cols(d_hidden, up_weight)
    dx_second, dgain_second, dbias_second = pull_second(d_second)
    d_context = dot_cols(cotangent, dense_weight).astype(jnp.bfloat16)
    d_context = d_context.reshape(seqs_here, LEN, heads_here, HS)

    def attend_back(seq_item):
        query_seq, key_seq, value_seq, segment_row, total_seq, dout_seq = seq_item
        query_grads = []
        key_grad = jnp.zeros(key_seq.shape, jnp.float32)
        value_grad = jnp.zeros(value_seq.shape, jnp.float32)
        for row_start in range(0, LEN, block_rows):
            query_block = query_seq[row_start : row_start + block_rows]
            dout_block = dout_seq[row_start : row_start + block_rows]
            scores = masked_scores(query_block, key_seq, segment_row, row_start, score_scale)
            attn_probs = jnp.exp(scores - total_seq[:, row_start : row_start + block_rows])
            d_probs = jnp.einsum(
                "qhd,khd->hqk", dout_block, value_seq, preferred_element_type=jnp.float32
            )
            inner = jnp.sum(attn_probs * d_probs, axis=-1, keepdims=True)
            d_scores = (attn_probs * (d_probs - inner)).astype(jnp.bfloat16)
            query_grads.append(
                jnp.einsum("hqk,khd->qhd", d_scores, key_seq, preferred_element_type=jnp.float32)
                * score_scale
            )
            key_grad = (
                key_grad
                + jnp.einsum(
                    "hqk,qhd->khd", d_scores, query_block, preferred_element_type=jnp.float32
                )
                * score_scale
            )
            value_grad = value_grad + jnp.einsum(
                "hqk,qhd->khd",
                attn_probs.astype(jnp.bfloat16),
                dout_block,
                preferred_element_type=jnp.float32,
            )
        return (jnp.concatenate(query_grads, axis=0), key_grad, value_grad)

    query_grad, key_grad, value_grad = lax.map(
        attend_back, (queries, key_rows, values, segments, log_totals, d_context)
    )
    d_joined = jnp.stack([pull_turn(query_grad)[0], pull_turn(key_grad)[0], value_grad], axis=3)
    d_joined = d_joined.reshape(rows_here, 3 * heads_here * HS).astype(jnp.bfloat16)
    qkv_bias_grad = jnp.sum(d_joined, axis=0, dtype=jnp.float32)
    d_first = dot_cols(d_joined, qkv_weight)
    dx_first, dgain_first, dbias_first = pull_first(d_first)
    qkv_part, dense_part, up_part, down_part = (
        lax.psum_scatter(dot_rows(first_norm, d_joined), "dp", scatter_dimension=0, tiled=True),
        lax.psum_scatter(dense_grad, "dp", scatter_dimension=1, tiled=True),
        lax.psum_scatter(dot_rows(second_norm, d_hidden), "dp", scatter_dimension=0, tiled=True),
        lax.psum_scatter(down_grad, "dp", scatter_dimension=1, tiled=True),
    )
    norm_part = jnp.stack([dgain_first, dbias_first, dgain_second, dbias_second], axis=0)
    input_sum, norm_group = lax.psum((dx_first + dx_second, norm_part), "tensor")
    bias_qkv, bias_up, bias_out, norm_total = lax.psum(
        (qkv_bias_grad, up_bias_grad, out_bias_grad, norm_group), "dp"
    )
    input_grad = (grad_full + input_sum).astype(jnp.bfloat16)
    widths = jnp.array([HEADS * HS, FF], jnp.float32)
    subset_rms = jnp.sqrt(
        stats_total[:, :2] / (jnp.maximum(stats_total[:, 2:3], 1.0) * widths[None, :])
    )
    return (
        out,
        input_grad,
        norm_total[0],
        norm_total[1],
        qkv_part,
        bias_qkv,
        dense_part,
        bias_out,
        norm_total[2],
        norm_total[3],
        up_part,
        bias_up,
        down_part,
        bias_out,
        subset_rms,
    )


def solution(mesh):
    placed = (
        P("dp", None),
        P("dp", None),
        P("dp", None),
        P("dp"),
        P(),
        P(),
        P(None, "tensor"),
        P("tensor"),
        P("tensor", None),
        P(),
        P(),
        P(),
        P(None, "tensor"),
        P("tensor"),
        P("tensor", None),
        P(),
    )
    return jax.shard_map(
        on_device,
        mesh=mesh,
        in_specs=placed,
        out_specs=(
            P("dp", None),
            P("dp", None),
            P(),
            P(),
            P("dp", "tensor"),
            P("tensor"),
            P("tensor", "dp"),
            P(),
            P(),
            P(),
            P("dp", "tensor"),
            P("tensor"),
            P("tensor", "dp"),
            P(),
            P(),
        ),
        check_vma=False,
    )
```

profile of v0, /device:TPU:10, one launch (start us, length us, event | category | flops | bytes accessed | tf_op | source)
XLA Modules:
  0.0 826.4 jit_solution(14295815886303257674)
XLA Ops:
  8.1 3.0 convert_reduce_fusion
  11.1 0.5 copy-done.1
  11.7 1.2 fusion.17
  12.9 0.6 copy-done.10
  13.5 11.6 %convolution_add_fusion = f32[1024,1536]{1,0:T(8,128)} fusion(bf16[2048,1536]{1,0:T(8,128)(2,1)} %param.23, f32[1536]{0:T(1024)S(1)} %copy-done.23, bf16[1024,2048]{1,0:T(8,128)(2,1)S(1)} %copy-done.1, f32[2048]{0:T(1024)S(1)} %copy-done.25, f32[2048]{0:T(1024)S(1)} %copy-done.12, f32[1024]{0:T(1024)S(1)} %fusion.61, f32[1024]{0:T(1024)S(1)} %broadcast_multiply_fusion), kind=kOutput, calls=%fused_computation.52 | convolution fusion | flops 6456606720 | bytes 16807936 | tf_op jit(solution)/shard_map/dot_general | solution.py:95
  25.1 6.5 copy.68
  31.7 4.8 fusion.78
  36.5 2.9 copy.103
  39.4 2.0 fusion.49
  41.3 2.9 copy.102
  44.2 2.0 slice.172
  46.2 3.0 slice_negate_fusion.2
  49.4 2.2 fusion.60
  51.6 1.2 fusion.41
  52.8 0.7 fusion.57
  53.6 1.6 fusion.84
  55.2 1.1 fusion.30
  56.4 2.4 bitcast_convert_fusion
  59.1 2.4 convolution_convert_fusion
  61.6 1.3 fusion.34
  62.9 1.4 multiply_reduce_fusion.1
  64.3 1.6 fusion.85
  65.9 1.1 fusion.29
  67.1 2.3 bitcast_convert_fusion.1
  69.3 1.7 multiply_reduce_fusion.2
  71.1 0.8 multiply_convert_fusion.1
  71.9 0.8 fusion.48
  72.8 1.1 fusion.63
  73.9 0.8 multiply_convert_fusion
  74.8 0.8 fusion.47
  75.6 1.2 multiply_bitcast_fusion
  76.8 0.6 split.36
  77.7 0.6 split.32
  78.3 1.3 add_bitcast_fusion
  80.4 0.7 pad_add_fusion.1
  81.1 0.5 add_bitcast_fusion.1
  81.6 0.5 add_bitcast_fusion.2
  82.1 2.7 convert_reduce_fusion.3
  84.8 4.7 copy.86
  89.5 34.8 %multiply_reduce_fusion = (f32[]{:T(128)}, f32[1024,2048]{1,0:T(8,128)}, f32[1024,2048]{1,0:T(8,128)}) fusion(f32[2048]{0:T(1024)S(1)} %copy-done.24, bf16[2048,2048]{1,0:T(8,128)(2,1)} %param.29, bf16[1024,2048]{1,0:T(8,128)(2,1)} %param.17, f32[2048]{0:T(1024)S(1)} %copy-done.27, f32[2048]{0:T(1024)S(1)} %copy-done.14, f32[1024]{0:T(1024)S(1)} %fusion.61, ...), kind=kOutput, calls=%fused_computation.32 | convolution fusion | flops 8743026688 | bytes 29392900 | tf_op jit(solution)/shard_map/dot_general | solution.py:131
  124.3 21.9 %convert_reduce_fusion.2 = (f32[2048]{0:T(1024)}, bf16[1024,2048]{1,0:T(8,128)(2,1)}, bf16[1024,2048]{1,0:T(8,128)(2,1)}) fusion(f32[1024,2048]{1,0:T(8,128)} %get-tuple-element.84, f32[1024,2048]{1,0:T(8,128)} %get-tuple-element.122, f32[2048]{0:T(1024)S(1)} %copy-done.24, bf16[1024,2048]{1,0:T(8,128)(2,1)} %param.18, bf16[2048,2048]{1,0:T(8,128)(2,1)} %param.31), kind=kOutput, calls=%fused_computation.33 | convolution fusion | flops 8629778432 | bytes 37765120 | tf_op jit(solution)/shard_map/dot_general | solution.py:50
  146.2 12.7 %fusion.91 = f32[1024,2048]{1,0:T(8,128)S(1)} fusion(bf16[1024,2048]{1,0:T(8,128)(2,1)} %get-tuple-element.86, bf16[2048,2048]{1,0:T(8,128)(2,1)} %param.29), kind=kOutput, calls=%fused_computation.163 | convolution fusion | flops 8589934592 | bytes 20971520 | tf_op jit(solution)/shard_map/dot_general | solution.py:50
  158.9 13.9 %fusion.18 = (f32[1024]{0:T(1024)}, f32[1024]{0:T(1024)}, f32[1024,2048]{1,0:T(8,128)}) fusion(bf16[1024,2048]{1,0:T(8,128)(2,1)S(1)} %copy-done.2, f32[2048]{0:T(1024)} %param.21, f32[1024]{0:T(1024)S(1)} %broadcast_multiply_fusion, f32[1024,2048]{1,0:T(8,128)S(1)} %fusion.91, f32[2048]{0:T(1024)} %param.27, bf16[1024,1536]{0,1:T(8,128)(2,1)S(1)} %bitcast.125, ...), kind=kOutput, calls=%fused_computation.26 | convolution fusion | flops 6459226112 | bytes 30437376 | tf_op jit(solution)/shard_map/dot_general | solution.py:50
  172.9 0.7 multiply_multiply_fusion.6
  173.6 9.5 %fusion.15 = (f32[2048]{0:T(1024)S(1)}, f32[1024]{0:T(1024)S(1)}, f32[2048]{0:T(1024)S(1)}, f32[2048]{0:T(1024)S(1)}, f32[1024]{0:T(1024)S(1)}, /*index=5*/f32[2048]{0:T(1024)S(1)}) fusion(f32[1024,2048]{1,0:T(8,128)} %get-tuple-element.135, bf16[1024,2048]{1,0:T(8,128)(2,1)S(1)} %copy-done.2, f32[1024]{0:T(1024)S(1)} %fusion.61, ...), kind=kLoop, calls=%fused_computation.23 | loop fusion | flops 44029952 | bytes 21045248 | tf_op jit(solution)/shard_map/transpose(jvp())/reduce_sum | solution.py:21
  183.1 13.4 %fusion.90 = f32[1024,2048]{1,0:T(8,128)} fusion(bf16[1024,2048]{1,0:T(8,128)(2,1)S(1)} %copy-done.29, bf16[2048,2048]{1,0:T(8,128)(2,1)} %param.31), kind=kOutput, calls=%fused_computation.162 | convolution fusion | flops 8589934592 | bytes 20971520 | tf_op jit(solution)/shard_map/dot_general | solution.py:134
  196.7 6.9 add_add_fusion.2
  203.6 9.0 %convolution_add_fusion.1 = f32[1024,2048]{1,0:T(8,128)} fusion(f32[1024,2048]{1,0:T(8,128)} %fusion.90, bf16[1024,512]{0,1:T(8,128)(2,1)S(1)} %bitcast.118, bf16[512,2048]{1,0:T(8,128)(2,1)S(1)} %copy-done), kind=kOutput, calls=%fused_computation.65 | convolution fusion | flops 2149580800 | bytes 19922944 | tf_op jit(solution)/shard_map/dot_general | solution.py:128
  212.7 6.5 fusion.92
  219.3 15.2 %fusion.72 = f32[2048,1536]{1,0:T(8,128)} fusion(bf16[1024,1536]{0,1:T(8,128)(2,1)} %bitcast.124, bf16[1024,2048]{1,0:T(8,128)(2,1)} %param.17, f32[2048]{0:T(1024)S(1)} %copy-done.26, f32[2048]{0:T(1024)S(1)} %copy-done.13, f32[1024]{0:T(1024)S(1)} %fusion.61, f32[1024]{0:T(1024)S(1)} %broadcast_multiply_fusion), kind=kOutput, calls=%fused_computation.151 | convolution fusion | flops 6455033856 | bytes 19947520 | tf_op jit(solution)/shard_map/dot_general | solution.py:44
  234.6 0.6 copy-done.28
  235.2 16.0 %fusion.68 = f32[2048,2048]{1,0:T(8,128)} fusion(bf16[1024,2048]{1,0:T(8,128)(2,1)} %get-tuple-element.86, bf16[1024,2048]{1,0:T(8,128)(2,1)} %param.17, f32[2048]{0:T(1024)S(1)} %copy-done.28, f32[2048]{0:T(1024)S(1)} %copy-done.15, f32[1024]{0:T(1024)S(1)} %fusion.61, f32[1024]{0:T(1024)S(1)} %broadcast_multiply_fusion), kind=kOutput, calls=%fused_computation.149 | convolution fusion | flops 8602517504 | bytes 25190400 | tf_op jit(solution)/shard_map/dot_general | solution.py:44
  251.3 15.3 %fusion.93 = f32[2048,2048]{1,0:T(8,128)} fusion(bf16[1024,2048]{1,0:T(8,128)(2,1)} %get-tuple-element.89, bf16[1024,2048]{1,0:T(8,128)(2,1)} %param.18), kind=kOutput, calls=%fused_computation.165 | convolution fusion | flops 8589934592 | bytes 25165824 | tf_op jit(solution)/shard_map/dot_general | solution.py:44
  267.8 2.4 fusion.38
  270.2 1.4 maximum_bitcast_fusion.1
  271.6 48.7 %psum.63 = f32[22,3]{0,1:T(4,128)S(1)} all-reduce(f32[22,3]{0,1:T(4,128)S(1)} %broadcast_multiply_fusion.1), channel_id=1, replica_groups=mesh['dp'=8,'tensor'=4] {'dp','tensor'}, use_global_device_ids=true, to_apply=%region_32.33 | all-reduce | flops 66 | bytes 528 | tf_op jit(solution)/shard_map/psum | solution.py:145
  320.4 21.2 %psum.58 = f32[4,2048]{1,0:T(4,128)S(1)} all-reduce(f32[4,2048]{1,0:T(4,128)S(1)} %pad_maximum_fusion.4), channel_id=1, replica_groups=mesh['dp'=8,'tensor'=4] {'tensor'}, use_global_device_ids=true, to_apply=%region_18.19 | all-reduce | flops 8192 | bytes 65536 | tf_op jit(solution)/shard_map/psum | solution.py:207
  341.6 0.6 fusion.62
  342.2 435.1 %all-reduce.12.cloned.1.call-done = (f32[1024,2048]{1,0:T(8,128)}, f32[1024,2048]{1,0:T(8,128)}) async-done(((f32[1024,2048]{1,0:T(8,128)}, f32[1024,2048]{1,0:T(8,128)}), (f32[1024,2048]{1,0:T(8,128)}, f32[1024,2048]{1,0:T(8,128)})) %all-reduce.12.cloned.1.call-update) | async-done | bytes 16777232 | tf_op jit(solution)/shard_map/psum | solution.py:135
  777.3 8.8 %convert_reduce_fusion.1 = (f32[2048]{0:T(1024)S(1)}, bf16[1024,2048]{1,0:T(8,128)(2,1)}) fusion(bf16[1024,2048]{1,0:T(8,128)(2,1)} %param.18, f32[1024,2048]{1,0:T(8,128)} %get-tuple-element.82), kind=kLoop, calls=%fused_computation.16 | loop fusion | flops 8386560 | bytes 16785408 | tf_op jit(solution)/shard_map/reduce_sum | solution.py:147
  786.1 22.5 %all-reduce.8 = (f32[4,2048]{1,0:T(4,128)S(1)}, f32[1536]{0:T(1024)}, f32[2048]{0:T(1024)S(1)}, f32[2048]{0:T(1024)}) all-reduce(f32[4,2048]{1,0:T(4,128)S(1)} %psum.58, f32[1536]{0:T(1024)S(1)} %reduce_sum.207, f32[2048]{0:T(1024)S(1)} %get-tuple-element.92, f32[2048]{0:T(1024)S(1)} %copy-done.20), channel_id=1, replica_groups=mesh['dp'=8,'tensor'=4] {'dp'}, use_global_device_ids=true, to_apply=%region_19.20 | all-reduce | flops 13824 | bytes 110592 | tf_op jit(solution)/shard_map/psum | solution.py:208
  808.6 0.6 fusion.82
  809.3 8.4 %fusion.22 = bf16[1024,2048]{1,0:T(8,128)(2,1)} fusion(f32[1024,2048]{1,0:T(8,128)} %get-tuple-element.81, bf16[1024,2048]{1,0:T(8,128)(2,1)} %param.17, f32[2048]{0:T(1024)S(1)} %copy-done.18, f32[2048]{0:T(1024)S(1)} %copy-done.19), kind=kLoop, calls=%fused_computation.30 | loop fusion | flops 10485760 | bytes 16793600 | tf_op jit(solution)/shard_map/convert_element_type | solution.py:136
  817.7 0.6 copy.116
  (103 shorter events, 2.7 us)
Async XLA Ops:
  8.0 50.8 %copy-start = (bf16[512,2048]{1,0:T(8,128)(2,1)S(1)}, bf16[512,2048]{1,0:T(8,128)(2,1)}, u32[]{:S(2)}) copy-start(bf16[512,2048]{1,0:T(8,128)(2,1)} %param.25) | copy-start | bytes 6291460
  8.0 5.5 copy-start.12
  8.0 769.3 %all-reduce.12.cloned.1.call-start = ((), (), s32[]{:S(2)}) async-start(), calls=%async_computation.8 | async-start | bytes 33554432 | tf_op jit(solution)/shard_map/psum | solution.py:135
  8.1 3.6 copy-start.1
  8.1 5.4 copy-start.23
  8.1 5.4 copy-start.25
  12.9 0.6 copy-start.10
  44.2 5.0 copy-start.17
  46.2 6.6 copy-start.3
  46.2 6.6 copy-start.4
  52.8 3.5 slice-start
  53.6 2.8 slice-start.1
  56.4 2.8 copy-start.5
  82.1 7.4 copy-start.14
  82.1 7.4 copy-start.24
  82.1 7.4 copy-start.27
  146.2 12.7 %copy-start.2 = (bf16[1024,2048]{1,0:T(8,128)(2,1)S(1)}, bf16[1024,2048]{1,0:T(8,128)(2,1)}, u32[]{:S(2)}) copy-start(bf16[1024,2048]{1,0:T(8,128)(2,1)} %param.17) | copy-start | bytes 12582916
  146.2 12.7 %copy-start.6 = (bf16[1,1024,2,3,256]{1,4,3,2,0:T(8,128)(2,1)S(1)}, bf16[1,1024,2,3,256]{1,4,3,2,0:T(8,128)(2,1)}, u32[]{:S(2)}) copy-start(bf16[1,1024,2,3,256]{1,4,3,2,0:T(8,128)(2,1)} %copy.86) | copy-start | bytes 9437188
  158.9 14.0 %copy-start.11 = (f32[1024]{0:T(1024)S(1)}, f32[1024]{0:T(1024)}, u32[]{:S(2)}) copy-start(f32[1024]{0:T(1024)} %copy-done.10) | copy-start | bytes 12292
  173.6 9.5 %copy-start.29 = (bf16[1024,2048]{1,0:T(8,128)(2,1)S(1)}, bf16[1024,2048]{1,0:T(8,128)(2,1)}, u32[]{:S(2)}) copy-start(bf16[1024,2048]{1,0:T(8,128)(2,1)} %get-tuple-element.89) | copy-start | bytes 12582916
  183.1 13.6 %slice-start.2 = ((s8[8388608]{0:T(1024)(128)(4,1)}), s8[4194304]{0:T(1024)(128)(4,1)S(1)}, s32[]{:S(2)}) async-start(s8[8388608]{0:T(1024)(128)(4,1)} %bitcast.110), calls=%async_computation.11 | async-start | bytes 8388608
  183.1 13.4 %copy-start.8 = (bf16[512,2,256]{0,2,1:T(8,128)(2,1)S(1)}, bf16[512,2,256]{0,2,1:T(8,128)(2,1)}, u32[]{:S(2)}) copy-start(bf16[512,2,256]{0,2,1:T(8,128)(2,1)} %get-tuple-element.125) | copy-start | bytes 1572868
  183.1 13.4 %copy-start.9 = (bf16[512,2,256]{0,2,1:T(8,128)(2,1)S(1)}, bf16[512,2,256]{0,2,1:T(8,128)(2,1)}, u32[]{:S(2)}) copy-start(bf16[512,2,256]{0,2,1:T(8,128)(2,1)} %get-tuple-element.129) | copy-start | bytes 1572868
  183.1 13.6 %slice-start.3 = ((s8[8388608]{0:T(1024)(128)(4,1)}), s8[4194304]{0:T(1024)(128)(4,1)S(1)}, s32[]{:S(2)}) async-start(s8[8388608]{0:T(1024)(128)(4,1)} %bitcast.110), calls=%async_computation.12 | async-start | bytes 8388608
  183.1 13.6 %copy-start.13 = (f32[2048]{0:T(1024)S(1)}, f32[2048]{0:T(1024)}, u32[]{:S(2)}) copy-start(f32[2048]{0:T(1024)} %param.21) | copy-start | bytes 24580
  183.1 13.5 %copy-start.15 = (f32[2048]{0:T(1024)S(1)}, f32[2048]{0:T(1024)}, u32[]{:S(2)}) copy-start(f32[2048]{0:T(1024)} %param.27) | copy-start | bytes 24580
  212.7 6.6 copy-start.26
  212.7 605.0 %reduce-scatter.7.cloned.1.call-start = ((), (), s32[]{:S(2)}) async-start(), calls=%async_computation.5 | async-start | bytes 4718592 | tf_op jit(solution)/shard_map/reduce_scatter | solution.py:202
  219.2 598.4 %reduce-scatter.5.cloned.1.call-start = ((), (), s32[]{:S(2)}) async-start(), calls=%async_computation.4 | async-start | bytes 14155776 | tf_op jit(solution)/shard_map/reduce_scatter | solution.py:201
  234.5 0.7 copy-start.28
  234.5 583.1 %reduce-scatter.9.cloned.1.call-start = ((), (), s32[]{:S(2)}) async-start(), calls=%async_computation.6 | async-start | bytes 18874368 | tf_op jit(solution)/shard_map/reduce_scatter | solution.py:203
  251.2 566.5 %reduce-scatter.11.cloned.1.call-start = ((), (), s32[]{:S(2)}) async-start(), calls=%async_computation.7 | async-start | bytes 18874368 | tf_op jit(solution)/shard_map/reduce_scatter | solution.py:204
  266.6 0.8 copy-start.16
  266.6 1.3 copy-start.7
  266.6 75.0 %copy-start.22 = (f32[2]{0:T(128)S(1)}, f32[2]{0:T(128)}, u32[]{:S(2)}) copy-start(f32[2]{0:T(128)} %constant.146.clone) | copy-start | bytes 28
  777.3 8.8 %copy-start.20 = (f32[2048]{0:T(1024)S(1)}, f32[2048]{0:T(1024)}, u32[]{:S(2)}) copy-start(f32[2048]{0:T(1024)} %get-tuple-element.85) | copy-start | bytes 24580
  777.3 32.0 %copy-start.18 = (f32[2048]{0:T(1024)S(1)}, f32[2048]{0:T(1024)}, u32[]{:S(2)}) copy-start(f32[2048]{0:T(1024)} %param.32) | copy-start | bytes 24580
  777.3 32.0 %copy-start.19 = (f32[2048]{0:T(1024)S(1)}, f32[2048]{0:T(1024)}, u32[]{:S(2)}) copy-start(f32[2048]{0:T(1024)} %param.26) | copy-start | bytes 24580
  808.6 9.1 %copy-start.21 = (f32[2048]{0:T(1024)}, f32[2048]{0:T(1024)S(1)}, u32[]{:S(2)}) copy-start(f32[2048]{0:T(1024)S(1)} %get-tuple-element.166) | copy-start | bytes 24580
Sparse Core Ops, SparseCore 0:
  212.8 564.4 all-reduce.11
Sparse Core Ops, SparseCore 1:
  219.3 52.2 reduce-scatter.6
  276.0 92.7 reduce-scatter.4
  373.2 115.8 reduce-scatter.8
  493.7 115.7 reduce-scatter.10
where the time goes:
time: 842 us; the launch traced here: 826 us
  waiting for transfers between devices  435 us (52%)
  matrix products  190 us (23%)
  blocking collectives  92.4 us (11%)
  other arithmetic  59.8 us (7%)
  local copies, waits for them, and re-layouts  30.9 us (4%)
  between operations  17.5 us (2%)
    psum x1, waiting for transfers between devices, on_device(): branches = lax.psum(branch_terms, 'tensor')  435 us
    dot_general x4, matrix products, dot_rows(): lax.dot_general(left, right, (((0,), (0,)), ((), ())), preferred_element_...  53 us
    dot_general x4, matrix products, dot_cols(): lax.dot_general(left, right, (((1,), (1,)), ((), ())), preferred_element_...  50.9 us
    psum x1, blocking collectives, on_device(): stats_total = lax.psum(stats_local, ('dp', 'tensor'))  48.7 us
    dot_general x1, matrix products, on_device(): jnp.dot(second_norm, up_weight, preferred_element_type=jnp.float32)  34.8 us
    psum x1, blocking collectives, on_device(): lax.psum((qkv_bias_grad, up_bias_grad, out_bias_grad, norm_group), 'dp')  22.5 us
    psum x1, blocking collectives, on_device(): lax.psum((dx_first + dx_second, norm_part), 'tensor')  21.2 us
  transfers between devices with their start and end apart: 5, of which 1 were waited for; matrix products, arithmetic and copies ran while one was open for 9% of the time, Pallas kernels for 0%

commit v1 on v0

--- a/solution.py
+++ b/solution.py
@@ -1,6 +1,9 @@
+import functools
 import jax
 import jax.numpy as jnp
 from jax import lax
+from jax.experimental import pallas as pl
+from jax.experimental.pallas import tpu as pltpu
 from jax.sharding import PartitionSpec as P
 
 HEADS = 8
@@ -13,6 +16,83 @@
 
 EPSILON = 1e-05
 MASKED_SCORE = -1000000000.0
+
+MESH=pl.DeviceIdType.MESH
+CH=32; W=8; H=4
+def line_kernel(n, p_ref, o_ref, near_in, far_in, own, low, s1, r1, s2, r2, lp, lo):
+    d=lax.axis_index("dp"); t=lax.axis_index("tensor")
+    near=t+1-2*lax.rem(t,2); far=3-t
+    mid=(t==1)|(t==2)
+    bar=pltpu.get_barrier_semaphore()
+    pl.semaphore_signal(bar,inc=1,device_id=(d,near),device_id_type=MESH)
+    @pl.when(mid)
+    def _():
+        pl.semaphore_signal(bar,inc=1,device_id=(d,far),device_id_type=MESH)
+        pl.semaphore_wait(bar,2)
+    @pl.when(jnp.logical_not(mid))
+    def _():
+        pl.semaphore_wait(bar,1)
+    def rows(k): return pl.ds(pl.multiple_of(k*CH,CH),CH)
+    def slot(k): return lax.rem(k,W)
+    def send_part(k):
+        return pltpu.make_async_remote_copy(src_ref=p_ref.at[rows(k)],dst_ref=near_in.at[slot(k)],send_sem=s1.at[slot(k)],recv_sem=r1.at[slot(k)],device_id=(d,near),device_id_type=MESH)
+    def swap(k):
+        return pltpu.make_async_remote_copy(src_ref=near_in.at[slot(k)],dst_ref=far_in.at[slot(k)],send_sem=s2.at[slot(k)],recv_sem=r2.at[slot(k)],device_id=(d,far),device_id_type=MESH)
+    def send_sum(k):
+        return pltpu.make_async_remote_copy(src_ref=far_in.at[slot(k)],dst_ref=near_in.at[slot(k)],send_sem=s1.at[slot(k)],recv_sem=r1.at[slot(k)],device_id=(d,near),device_id_type=MESH)
+    def load_own(k):
+        return pltpu.make_async_copy(p_ref.at[rows(k)],own.at[lax.rem(k,2)],lp.at[lax.rem(k,2)])
+    def store(k):
+        return pltpu.make_async_copy(low.at[lax.rem(k,2)],o_ref.at[rows(k)],lo.at[lax.rem(k,2)])
+    def emit(k,ref):
+        @pl.when(k>=2)
+        def _(): store(k-2).wait()
+        low[lax.rem(k,2)]=ref[slot(k)].astype(jnp.bfloat16)
+        store(k).start()
+    @pl.when(jnp.logical_not(mid))
+    def _():
+        @pl.loop(0,W)
+        def _(k): send_part(k).start()
+        @pl.loop(0,n)
+        def _(k):
+            send_sum(k).wait_recv()
+            send_part(k).wait_send()
+            emit(k,near_in)
+            @pl.when(k+W<n)
+            def _(): send_part(k+W).start()
+    @pl.when(mid)
+    def _():
+        load_own(0).start(); load_own(1).start()
+        @pl.loop(0,n+1)
+        def _(k):
+            @pl.when(k<n)
+            def _():
+                send_part(k).wait_recv()
+                load_own(k).wait()
+                near_in[slot(k)]=near_in[slot(k)]+own[lax.rem(k,2)]
+                @pl.when(k>=H)
+                def _(): send_sum(k-H).wait_send()
+                swap(k).start()
+                @pl.when(k+2<n)
+                def _(): load_own(k+2).start()
+            @pl.when(k>=1)
+            def _():
+                j=k-1
+                swap(j).wait()
+                far_in[slot(j)]=near_in[slot(j)]+far_in[slot(j)]
+                send_sum(j).start()
+                emit(j,far_in)
+        @pl.loop(n-H,n)
+        def _(k): send_sum(k).wait_send()
+    store(n-2).wait(); store(n-1).wait()
+def line_sum(p, cid=0):
+    rows,cols=p.shape
+    return pl.pallas_call(functools.partial(line_kernel,rows//CH),
+        out_shape=jax.ShapeDtypeStruct((rows,cols),jnp.bfloat16),
+        in_specs=[pl.BlockSpec(memory_space=pl.ANY)],out_specs=pl.BlockSpec(memory_space=pl.ANY),
+        scratch_shapes=[pltpu.VMEM((W,CH,cols),jnp.float32),pltpu.VMEM((W,CH,cols),jnp.float32),pltpu.VMEM((2,CH,cols),jnp.float32),pltpu.VMEM((2,CH,cols),jnp.bfloat16),
+          pltpu.SemaphoreType.DMA((W,)),pltpu.SemaphoreType.DMA((W,)),pltpu.SemaphoreType.DMA((W,)),pltpu.SemaphoreType.DMA((W,)),pltpu.SemaphoreType.DMA((2,)),pltpu.SemaphoreType.DMA((2,))],
+        compiler_params=pltpu.CompilerParams(collective_id=cid,has_side_effects=True,vmem_limit_bytes=40*2**20),name="line_sum")(p)
 
 
 def layer_norm(resid, norm_gain, norm_bias):
@@ -132,8 +212,8 @@
     active, pull_active = jax.vjp(gelu_exact, hidden)
     active_low = active.astype(jnp.bfloat16)
     branch_terms = attn_part + jnp.dot(active_low, down_weight, preferred_element_type=jnp.float32)
-    branches = lax.psum(branch_terms, "tensor")
-    out = (resid + branches + dense_bias + down_bias).astype(jnp.bfloat16)
+    first_here = lax.axis_index("tensor") == 1
+    out_terms = branch_terms + jnp.where(first_here, resid + (dense_bias + down_bias), 0.0)
     context_seq = jnp.sum((context * context).reshape(seqs_here, -1), axis=1)
     active_seq = jnp.sum((active * active).reshape(seqs_here, -1), axis=1)
     count_seq = jnp.where(lax.axis_index("tensor") == 0, float(LEN), 0.0) * jnp.ones_like(
@@ -204,11 +284,13 @@
         lax.psum_scatter(down_grad, "dp", scatter_dimension=1, tiled=True),
     )
     norm_part = jnp.stack([dgain_first, dbias_first, dgain_second, dbias_second], axis=0)
-    input_sum, norm_group = lax.psum((dx_first + dx_second, norm_part), "tensor")
+    grad_terms = dx_first + dx_second + jnp.where(first_here, grad_full, 0.0)
+    sums = line_sum(jnp.concatenate([out_terms, grad_terms], axis=0))
+    out, input_grad = sums[:rows_here], sums[rows_here:]
+    norm_group = lax.psum(norm_part, "tensor")
     bias_qkv, bias_up, bias_out, norm_total = lax.psum(
         (qkv_bias_grad, up_bias_grad, out_bias_grad, norm_group), "dp"
     )
-    input_grad = (grad_full + input_sum).astype(jnp.bfloat16)
     widths = jnp.array([HEADS * HS, FF], jnp.float32)
     subset_rms = jnp.sqrt(
         stats_total[:, :2] / (jnp.maximum(stats_total[:, 2:3], 1.0) * widths[None, :])

time: 842 us -> 783 us (0.930)
  waiting for transfers between devices: 435 us -> 0.1 us
  Pallas kernels: 0 us -> 378 us
  local copies, waits for them, and re-layouts: 30.9 us -> 44.4 us
  blocking collectives: 92.4 us -> 81 us
    psum x1 -> x0, waiting for transfers between devices: 435 us -> none  [on_device(): branches = lax.psum(branch_terms, 'tensor')]
    pallas_call x0 -> x1, Pallas kernels: none -> 378 us  [line_sum(): pl.pallas_call(functools.partial(line_kernel, rows // CH), out_shape=jax....]
  transfers between devices with their start and end apart: 5 -> 4, of which waited for: 1 -> 0; matrix products, arithmetic and copies ran while one was open for 9% -> 30% of each run, Pallas kernels for 0% -> 49%
where the time goes in v1:
time: 783 us; the launch traced here: 773 us
  Pallas kernels  378 us (48%)
  matrix products  195 us (25%)
  blocking collectives  81 us (10%)
  other arithmetic  57.9 us (7%)
  local copies, waits for them, and re-layouts  44.4 us (6%)
  between operations  15.5 us (2%)
    pallas_call x1, Pallas kernels, line_sum(): pl.pallas_call(functools.partial(line_kernel, rows // CH), out_shape=jax....  378 us
    dot_general x4, matrix products, dot_cols(): lax.dot_general(left, right, (((1,), (1,)), ((), ())), preferred_element_...  57 us
    dot_general x4, matrix products, dot_rows(): lax.dot_general(left, right, (((0,), (0,)), ((), ())), preferred_element_...  50.5 us
    psum x1, blocking collectives, on_device(): stats_total = lax.psum(stats_local, ('dp', 'tensor'))  42.3 us
    dot_general x1, matrix products, on_device(): jnp.dot(second_norm, up_weight, preferred_element_type=jnp.float32)  34.7 us
    psum x1, blocking collectives, on_device(): lax.psum((qkv_bias_grad, up_bias_grad, out_bias_grad, norm_group), 'dp')  23.1 us
    reduce_sum x1, other arithmetic, on_device(): out_bias_grad = jnp.sum(grad_full, axis=0)  15.7 us
  transfers between devices with their start and end apart: 4, of which 0 were waited for; matrix products, arithmetic and copies ran while one was open for 30% of the time, Pallas kernels for 49%

profile of v1, /device:TPU:10, one launch (start us, length us, event | category | flops | bytes accessed | tf_op | source)
XLA Modules:
  0.0 773.0 jit_solution(18043324300671036037)
XLA Ops:
  7.3 3.0 convert_reduce_fusion
  10.8 1.2 fusion.17
  12.1 0.6 copy-done.28
  12.7 11.7 %convolution_add_fusion = f32[1024,1536]{1,0:T(8,128)} fusion(bf16[2048,1536]{1,0:T(8,128)(2,1)} %param.23, f32[1536]{0:T(1024)S(1)} %copy-done.42, bf16[1024,2048]{1,0:T(8,128)(2,1)S(1)} %copy-done.2, f32[2048]{0:T(1024)S(1)} %copy-done.43, f32[2048]{0:T(1024)S(1)} %copy-done.30, f32[1024]{0:T(1024)S(1)} %fusion.60, f32[1024]{0:T(1024)S(1)} %broadcast_multiply_fusion), kind=kOutput, calls=%fused_computation.51 | convolution fusion | flops 6456606720 | bytes 16807936 | tf_op jit(solution)/shard_map/dot_general | solution.py:175
  24.4 6.6 copy.68
  30.9 4.8 fusion.78
  35.7 2.9 copy.103
  38.6 2.9 fusion.48
  41.6 2.9 copy.102
  44.4 2.0 slice.180
  46.4 3.0 slice_negate_fusion.2
  49.6 2.2 fusion.59
  51.9 1.2 fusion.40
  53.1 0.7 fusion.56
  53.9 1.6 fusion.84
  55.5 1.0 fusion.29
  56.5 2.4 bitcast_convert_fusion
  59.0 1.6 fusion.85
  60.6 1.0 fusion.28
  61.7 2.1 bitcast_convert_fusion.1
  63.9 1.0 copy-done.22
  64.9 4.3 fusion.92
  69.4 4.7 convolution_convert_fusion
  74.2 2.8 multiply_reduce_fusion.1
  77.0 0.8 multiply_convert_fusion
  77.9 1.8 copy-done.8
  79.6 3.0 multiply_reduce_fusion.2
  82.6 0.8 multiply_convert_fusion.1
  83.8 1.1 fusion.62
  84.9 1.1 multiply_bitcast_fusion
  86.1 0.6 split.36
  86.7 0.8 fusion.46
  87.6 0.8 fusion.47
  88.6 0.6 split.32
  90.4 0.7 pad_add_fusion.1
  92.1 1.3 fusion.33
  93.4 1.3 add_bitcast_fusion
  94.7 2.6 convert_reduce_fusion.3
  97.3 4.7 copy.86
  102.0 14.4 %fusion.71 = f32[2048,1536]{1,0:T(8,128)} fusion(bf16[1024,1536]{0,1:T(8,128)(2,1)} %bitcast.120, bf16[1024,2048]{1,0:T(8,128)(2,1)} %param.17, f32[2048]{0:T(1024)S(1)} %copy-done.43, f32[2048]{0:T(1024)S(1)} %copy-done.30, f32[1024]{0:T(1024)S(1)} %fusion.60, f32[1024]{0:T(1024)S(1)} %broadcast_multiply_fusion), kind=kOutput, calls=%fused_computation.149 | convolution fusion | flops 6455033856 | bytes 19947520 | tf_op jit(solution)/shard_map/dot_general | solution.py:124
  117.2 34.7 %multiply_reduce_fusion = (f32[]{:T(128)}, f32[1024,2048]{1,0:T(8,128)}, f32[1024,2048]{1,0:T(8,128)}) fusion(f32[2048]{0:T(1024)S(1)} %copy-done.44, bf16[2048,2048]{1,0:T(8,128)(2,1)} %param.29, bf16[1024,2048]{1,0:T(8,128)(2,1)} %param.17, f32[2048]{0:T(1024)S(1)} %copy-done.45, f32[2048]{0:T(1024)S(1)} %copy-done.32, f32[1024]{0:T(1024)S(1)} %fusion.60, ...), kind=kOutput, calls=%fused_computation.32 | convolution fusion | flops 8743026688 | bytes 29392900 | tf_op jit(solution)/shard_map/dot_general | solution.py:211
  151.8 23.0 %convert_reduce_fusion.2 = (f32[2048]{0:T(1024)}, bf16[1024,2048]{1,0:T(8,128)(2,1)}, bf16[1024,2048]{1,0:T(8,128)(2,1)}) fusion(f32[1024,2048]{1,0:T(8,128)} %get-tuple-element.82, f32[1024,2048]{1,0:T(8,128)} %get-tuple-element.130, f32[2048]{0:T(1024)S(1)} %copy-done.44, bf16[1024,2048]{1,0:T(8,128)(2,1)} %param.18, bf16[2048,2048]{1,0:T(8,128)(2,1)} %param.31), kind=kOutput, calls=%fused_computation.33 | convolution fusion | flops 8629778432 | bytes 37765120 | tf_op jit(solution)/shard_map/dot_general | solution.py:130
  174.9 16.1 %fusion.67 = f32[2048,2048]{1,0:T(8,128)} fusion(bf16[1024,2048]{1,0:T(8,128)(2,1)} %get-tuple-element.84, bf16[1024,2048]{1,0:T(8,128)(2,1)} %param.17, f32[2048]{0:T(1024)S(1)} %copy-done.45, f32[2048]{0:T(1024)S(1)} %copy-done.32, f32[1024]{0:T(1024)S(1)} %fusion.60, f32[1024]{0:T(1024)S(1)} %broadcast_multiply_fusion), kind=kOutput, calls=%fused_computation.147 | convolution fusion | flops 8602517504 | bytes 25190400 | tf_op jit(solution)/shard_map/dot_general | solution.py:124
  191.0 15.8 %fusion.93 = f32[2048,2048]{1,0:T(8,128)} fusion(bf16[1024,2048]{1,0:T(8,128)(2,1)} %get-tuple-element.87, bf16[1024,2048]{1,0:T(8,128)(2,1)} %param.18), kind=kOutput, calls=%fused_computation.164 | convolution fusion | flops 8589934592 | bytes 25165824 | tf_op jit(solution)/shard_map/dot_general | solution.py:124
  207.5 0.6 reduce_sum.207
  208.1 12.8 %fusion.91 = f32[1024,2048]{1,0:T(8,128)S(1)} fusion(bf16[1024,2048]{1,0:T(8,128)(2,1)} %get-tuple-element.84, bf16[2048,2048]{1,0:T(8,128)(2,1)} %param.29), kind=kOutput, calls=%fused_computation.162 | convolution fusion | flops 8589934592 | bytes 20971520 | tf_op jit(solution)/shard_map/dot_general | solution.py:130
  221.0 16.4 %fusion.18 = (f32[1024]{0:T(1024)}, f32[1024]{0:T(1024)}, f32[1024,2048]{1,0:T(8,128)}) fusion(bf16[1024,2048]{1,0:T(8,128)(2,1)S(1)} %copy-done.3, f32[2048]{0:T(1024)} %param.21, f32[1024]{0:T(1024)S(1)} %broadcast_multiply_fusion, f32[1024,2048]{1,0:T(8,128)S(1)} %fusion.91, f32[2048]{0:T(1024)} %param.27, bf16[1024,1536]{0,1:T(8,128)(2,1)S(1)} %bitcast.121, ...), kind=kOutput, calls=%fused_computation.27 | convolution fusion | flops 6459226112 | bytes 30437376 | tf_op jit(solution)/shard_map/dot_general | solution.py:130
  237.4 0.7 multiply_multiply_fusion.6
  238.1 9.9 %fusion.15 = (f32[2048]{0:T(1024)S(1)}, f32[1024]{0:T(1024)S(1)}, f32[2048]{0:T(1024)S(1)}, f32[2048]{0:T(1024)S(1)}, f32[1024]{0:T(1024)S(1)}, /*index=5*/f32[2048]{0:T(1024)S(1)}) fusion(f32[1024,2048]{1,0:T(8,128)} %get-tuple-element.131, bf16[1024,2048]{1,0:T(8,128)(2,1)S(1)} %copy-done.3, f32[1024]{0:T(1024)S(1)} %fusion.60, ...), kind=kLoop, calls=%fused_computation.24 | loop fusion | flops 44029952 | bytes 21045248 | tf_op jit(solution)/shard_map/transpose(jvp())/reduce_sum | solution.py:101
  248.0 15.6 %psum.42 = f32[4,2048]{1,0:T(4,128)S(1)} all-reduce(f32[4,2048]{1,0:T(4,128)S(1)} %pad_maximum_fusion.5), channel_id=1, replica_groups=mesh['dp'=8,'tensor'=4] {'tensor'}, use_global_device_ids=true, to_apply=%region_16.17 | all-reduce | flops 8192 | bytes 65536 | tf_op jit(solution)/shard_map/psum | solution.py:290
  263.7 15.7 %convert_reduce_fusion.1 = (f32[2048]{0:T(1024)S(1)}, f32[1024,2048]{1,0:T(8,128)}) fusion(bf16[1024,2048]{1,0:T(8,128)(2,1)} %param.18, pred[]{:T(512)S(6)} %eq.101, f32[1024]{0:T(1024)S(1)} %negate_multiply_fusion.1, f32[1024]{0:T(1024)S(1)} %get-tuple-element.116, f32[1024,2048]{1,0:T(8,128)} %copy-done.9, f32[2048]{0:T(1024)S(1)} %copy-done.33, ...), kind=kLoop, calls=%fused_computation.17 | loop fusion | flops 39843840 | bytes 33603584 | tf_op jit(solution)/shard_map/reduce_sum | solution.py:227
  279.5 23.1 %all-reduce.8 = (f32[4,2048]{1,0:T(4,128)S(1)}, f32[1536]{0:T(1024)}, f32[2048]{0:T(1024)S(1)}, f32[2048]{0:T(1024)}) all-reduce(f32[4,2048]{1,0:T(4,128)S(1)} %psum.42, f32[1536]{0:T(1024)S(1)} %copy-done.34, f32[2048]{0:T(1024)S(1)} %get-tuple-element.92, f32[2048]{0:T(1024)S(1)} %copy-done.39), channel_id=1, replica_groups=mesh['dp'=8,'tensor'=4] {'dp'}, use_global_device_ids=true, to_apply=%region_17.18 | all-reduce | flops 13824 | bytes 110592 | tf_op jit(solution)/shard_map/psum | solution.py:291
  302.6 14.6 %fusion.90 = f32[1024,2048]{1,0:T(8,128)} fusion(bf16[1024,2048]{1,0:T(8,128)(2,1)} %get-tuple-element.87, bf16[2048,2048]{1,0:T(8,128)(2,1)} %param.31), kind=kOutput, calls=%fused_computation.161 | convolution fusion | flops 8589934592 | bytes 20971520 | tf_op jit(solution)/shard_map/dot_general | solution.py:214
  317.3 6.9 fusion.21
  324.1 6.4 pad_maximum_fusion.p_ref
  330.6 378.3 %line_sum.1 = bf16[2048,2048]{1,0:T(8,128)(2,1)S(1)} custom-call(f32[2048,2048]{1,0:T(8,128)} %pad_maximum_fusion.p_ref), custom_call_target="tpu_custom_call" | custom-call | tf_op jit(solution)/shard_map/line_sum/pallas_call | solution.py:90
  708.9 3.2 copy-done.1
  712.1 2.4 fusion.37
  714.5 1.4 maximum_bitcast_fusion.1
  715.9 42.3 %psum.47 = f32[22,3]{0,1:T(4,128)S(1)} all-reduce(f32[22,3]{0,1:T(4,128)S(1)} %broadcast_multiply_fusion.1), channel_id=1, replica_groups=mesh['dp'=8,'tensor'=4] {'dp','tensor'}, use_global_device_ids=true, to_apply=%region_30.31 | all-reduce | flops 66 | bytes 528 | tf_op jit(solution)/shard_map/psum | solution.py:225
  758.2 0.6 fusion.61
  758.9 0.6 fusion.82
  759.5 6.1 fusion.77
  765.7 0.6 copy.114
  (129 shorter events, 4.8 us)
Async XLA Ops:
  7.2 62.2 %copy-start = (bf16[512,2048]{1,0:T(8,128)(2,1)S(1)}, bf16[512,2048]{1,0:T(8,128)(2,1)}, u32[]{:S(2)}) copy-start(bf16[512,2048]{1,0:T(8,128)(2,1)} %param.25) | copy-start | bytes 6291460
  7.2 5.5 copy-start.30
  7.2 758.4 %reduce-scatter.7.cloned.1.call-start = ((), (), s32[]{:S(2)}) async-start(), calls=%async_computation.5 | async-start | bytes 4718592 | tf_op jit(solution)/shard_map/reduce_scatter | solution.py:282
  7.3 3.6 copy-start.2
  7.3 5.4 copy-start.42
  7.3 5.4 copy-start.43
  12.1 0.6 copy-start.28
  44.4 5.0 copy-start.36
  46.4 6.7 copy-start.11
  46.4 6.7 copy-start.12
  49.5 4.4 copy-start.24
  51.9 2.0 copy-start.13
  51.9 2.0 copy-start.15
  53.1 3.4 slice-start
  53.8 5.2 copy-start.17
  53.8 5.2 copy-start.26
  53.8 2.7 slice-start.1
  55.5 3.5 copy-start.5
  60.6 3.1 copy-start.7
  61.7 3.3 copy-start.19
  63.9 1.0 copy-start.22
  69.2 696.4 %reduce-scatter.5.cloned.1.call-start = ((), (), s32[]{:S(2)}) async-start(), calls=%async_computation.4 | async-start | bytes 14155776 | tf_op jit(solution)/shard_map/reduce_scatter | solution.py:281
  69.3 4.8 copy-start.6
  77.0 2.6 copy-start.8
  82.6 1.1 copy-start.18
  84.9 1.8 copy-start.25
  84.9 1.8 copy-start.27
  87.6 1.6 copy-start.16
  89.2 1.2 copy-start.14
  116.4 0.7 copy-start.32
  116.4 0.7 copy-start.44
  116.4 0.7 copy-start.45
  116.5 649.2 %reduce-scatter.9.cloned.1.call-start = ((), (), s32[]{:S(2)}) async-start(), calls=%async_computation.6 | async-start | bytes 18874368 | tf_op jit(solution)/shard_map/reduce_scatter | solution.py:283
  191.0 574.7 %reduce-scatter.11.cloned.1.call-start = ((), (), s32[]{:S(2)}) async-start(), calls=%async_computation.7 | async-start | bytes 18874368 | tf_op jit(solution)/shard_map/reduce_scatter | solution.py:284
  206.8 0.7 copy-start.35
  208.1 12.8 %copy-start.3 = (bf16[1024,2048]{1,0:T(8,128)(2,1)S(1)}, bf16[1024,2048]{1,0:T(8,128)(2,1)}, u32[]{:S(2)}) copy-start(bf16[1024,2048]{1,0:T(8,128)(2,1)} %param.17) | copy-start | bytes 12582916
  208.1 12.8 %copy-start.20 = (bf16[1,1024,2,3,256]{1,4,3,2,0:T(8,128)(2,1)S(1)}, bf16[1,1024,2,3,256]{1,4,3,2,0:T(8,128)(2,1)}, u32[]{:S(2)}) copy-start(bf16[1,1024,2,3,256]{1,4,3,2,0:T(8,128)(2,1)} %copy.86) | copy-start | bytes 9437188
  220.9 17.2 %copy-start.9 = (f32[1024,2048]{1,0:T(8,128)}, f32[1024,2048]{1,0:T(8,128)S(1)}, u32[]{:S(2)}) copy-start(f32[1024,2048]{1,0:T(8,128)S(1)} %fusion.91) | copy-start | bytes 25165828
  221.0 16.4 %copy-start.29 = (f32[1024]{0:T(1024)S(1)}, f32[1024]{0:T(1024)}, u32[]{:S(2)}) copy-start(f32[1024]{0:T(1024)} %copy-done.28) | copy-start | bytes 12292
  238.1 25.6 %copy-start.31 = (f32[2048]{0:T(1024)S(1)}, f32[2048]{0:T(1024)}, u32[]{:S(2)}) copy-start(f32[2048]{0:T(1024)} %param.21) | copy-start | bytes 24580
  238.1 25.6 %copy-start.33 = (f32[2048]{0:T(1024)S(1)}, f32[2048]{0:T(1024)}, u32[]{:S(2)}) copy-start(f32[2048]{0:T(1024)} %param.27) | copy-start | bytes 24580
  263.7 15.8 %copy-start.34 = (f32[1536]{0:T(1024)S(1)}, f32[1536]{0:T(1024)}, u32[]{:S(2)}) copy-start(f32[1536]{0:T(1024)} %reduce_sum.207) | copy-start | bytes 18436
  263.7 15.8 %copy-start.39 = (f32[2048]{0:T(1024)S(1)}, f32[2048]{0:T(1024)}, u32[]{:S(2)}) copy-start(f32[2048]{0:T(1024)} %get-tuple-element.83) | copy-start | bytes 24580
  263.7 38.9 %copy-start.37 = (f32[2048]{0:T(1024)S(1)}, f32[2048]{0:T(1024)}, u32[]{:S(2)}) copy-start(f32[2048]{0:T(1024)} %param.26) | copy-start | bytes 24580
  263.7 38.9 %copy-start.38 = (f32[2048]{0:T(1024)S(1)}, f32[2048]{0:T(1024)}, u32[]{:S(2)}) copy-start(f32[2048]{0:T(1024)} %param.32) | copy-start | bytes 24580
  302.6 463.1 %copy-start.40 = (f32[2048]{0:T(1024)}, f32[2048]{0:T(1024)S(1)}, u32[]{:S(2)}) copy-start(f32[2048]{0:T(1024)S(1)} %get-tuple-element.166) | copy-start | bytes 24580
  302.6 14.6 %copy-start.4 = (bf16[1024,2048]{1,0:T(8,128)(2,1)S(1)}, bf16[1024,2048]{1,0:T(8,128)(2,1)}, u32[]{:S(2)}) copy-start(bf16[1024,2048]{1,0:T(8,128)(2,1)} %param.17) | copy-start | bytes 12582916
  302.6 14.6 %copy-start.23 = (bf16[1024,2,256]{0,2,1:T(8,128)(2,1)S(1)}, bf16[1024,2,256]{0,2,1:T(8,128)(2,1)}, u32[]{:S(2)}) copy-start(bf16[1024,2,256]{0,2,1:T(8,128)(2,1)} %copy-done.22) | copy-start | bytes 3145732
  317.3 6.9 copy-start.10
  330.6 381.5 %copy-start.21 = (f32[2,256,512]{2,1,0:T(8,128)S(1)}, f32[2,256,512]{2,1,0:T(8,128)}, u32[]{:S(2)}) copy-start(f32[2,256,512]{2,1,0:T(8,128)} %get-tuple-element.133) | copy-start | bytes 3145732
  330.6 427.6 %copy-start.41 = (f32[2]{0:T(128)S(1)}, f32[2]{0:T(128)}, u32[]{:S(2)}) copy-start(f32[2]{0:T(128)} %constant.148.clone) | copy-start | bytes 28
  708.9 3.2 copy-start.1
Sparse Core Ops, SparseCore 0:
  69.4 52.3 reduce-scatter.6
  126.3 92.2 reduce-scatter.4
  223.2 117.1 reduce-scatter.8
  344.8 115.9 reduce-scatter.10

commit v2 on v0

--- a/solution.py
+++ b/solution.py
@@ -1,6 +1,9 @@
+import functools
 import jax
 import jax.numpy as jnp
 from jax import lax
+from jax.experimental import pallas as pl
+from jax.experimental.pallas import tpu as pltpu
 from jax.sharding import PartitionSpec as P
 
 HEADS = 8
@@ -13,6 +16,571 @@
 
 EPSILON = 1e-05
 MASKED_SCORE = -1000000000.0
+VMEM_ASK = 64 * 2**20
+
+MESH = pl.DeviceIdType.MESH
+F32 = jnp.float32
+LOW = jnp.bfloat16
+BLOCK = 256
+CH = 32
+PER = BLOCK // CH
+WINDOW = 8
+HELD = 4
+TILE = 512
+RSQRT2 = 0.7071067811865476
+RSQRT2PI = 0.3989422804014327
+SV = 8
+S_GAIN1, S_BIAS1, S_GAIN2, S_BIAS2, S_STATS, S_UP, S_QKV, S_OUT = range(SV)
+V_UP, V_GAIN1, V_GAIN2, V_BIAS2, V_OUT, V_PICK = range(6)
+
+
+def dot_nn(left, right):
+    return lax.dot_general(left, right, (((1,), (0,)), ((), ())), preferred_element_type=F32)
+
+
+def dot_nt(left, right):
+    return lax.dot_general(left, right, (((1,), (1,)), ((), ())), preferred_element_type=F32)
+
+
+def at_tile(index, width):
+    return pl.ds(pl.multiple_of(index * width, width), width)
+
+
+def layer_kernel(
+    ndp,
+    vec, sv0, x_h, cot_h, n1_h, ctx_h, dq_h, up_h, down_h, dense_h, qkv_h,
+    o_h, sv_o, gd_h, gu_h, p_h, n2_h, ad_h, au_h, bd_h, bu_h,
+    a_t, cot_v, dh_v, dq_v, ctx_v, sv_v, sq_v, svd, svz,
+    near_in, far_in, own, low,
+    s1, r1, s2, r2, lp, lo, lsem, wsem, psem, nsem,
+    ssv, rsv, ssz, rsz, sa, ra, sb, rb, ssem,
+):
+    d = lax.axis_index("dp")
+    t = lax.axis_index("tensor")
+    rows, cols = x_h.shape
+    ff = up_h.shape[1]
+    att = ctx_h.shape[1]
+    qw = dq_h.shape[1]
+    width = cols // ndp
+    half = ndp // 2
+    steps = rows // BLOCK
+    chunks = 2 * rows // CH
+    near = t + 1 - 2 * lax.rem(t, 2)
+    far = 3 - t
+    mid = (t == 1) | (t == 2)
+    end = jnp.logical_not(mid)
+    parity = lax.rem(d, 2)
+    mate = d + 1 - 2 * parity
+    here = lax.div(d, 2)
+    add_here = jnp.where(t == 1, 1.0, 0.0).astype(F32)
+
+    bar = pltpu.get_barrier_semaphore()
+    for k in range(1, 4):
+        pl.semaphore_signal(bar, inc=1, device_id=(d, lax.rem(t + k, 4)), device_id_type=MESH)
+
+    @pl.loop(1, ndp)
+    def _(k):
+        pl.semaphore_signal(bar, inc=1, device_id=(lax.rem(d + k, ndp), t), device_id_type=MESH)
+
+    def slot(k):
+        return lax.rem(k, WINDOW)
+
+    def send_part(k):
+        return pltpu.make_async_remote_copy(
+            src_ref=p_h.at[k], dst_ref=near_in.at[slot(k)], send_sem=s1.at[slot(k)],
+            recv_sem=r1.at[slot(k)], device_id=(d, near), device_id_type=MESH)
+
+    def swap(k):
+        return pltpu.make_async_remote_copy(
+            src_ref=near_in.at[slot(k)], dst_ref=far_in.at[slot(k)], send_sem=s2.at[slot(k)],
+            recv_sem=r2.at[slot(k)], device_id=(d, far), device_id_type=MESH)
+
+    def send_sum(k):
+        return pltpu.make_async_remote_copy(
+            src_ref=far_in.at[slot(k)], dst_ref=near_in.at[slot(k)], send_sem=s1.at[slot(k)],
+            recv_sem=r1.at[slot(k)], device_id=(d, near), device_id_type=MESH)
+
+    def load_own(k):
+        return pltpu.make_async_copy(p_h.at[k], own.at[lax.rem(k, 2)], lp.at[lax.rem(k, 2)])
+
+    def store(k):
+        return pltpu.make_async_copy(low.at[lax.rem(k, 2)], o_h.at[k], lo.at[lax.rem(k, 2)])
+
+    def emit(k, ref):
+        @pl.when(k >= 2)
+        def _():
+            store(k - 2).wait()
+
+        low[lax.rem(k, 2)] = ref[slot(k)].astype(LOW)
+        store(k).start()
+
+    LAG = 3
+
+    def prime():
+        @pl.when(end)
+        def _():
+            @pl.loop(0, WINDOW)
+            def _(k):
+                send_part(k).start()
+
+        @pl.when(mid)
+        def _():
+            load_own(0).start()
+            load_own(1).start()
+
+    def tick(k):
+        @pl.when(end & (k >= LAG) & (k < chunks + LAG))
+        def _():
+            j = k - LAG
+            send_sum(j).wait_recv()
+            send_part(j).wait_send()
+            emit(j, near_in)
+
+            @pl.when(j + WINDOW < chunks)
+            def _():
+                send_part(j + WINDOW).start()
+
+        @pl.when(mid & (k < chunks))
+        def _():
+            send_part(k).wait_recv()
+            load_own(k).wait()
+            near_in[slot(k)] = near_in[slot(k)] + own[lax.rem(k, 2)]
+
+            @pl.when(k >= HELD)
+            def _():
+                send_sum(k - HELD).wait_send()
+
+            swap(k).start()
+
+            @pl.when(k + 2 < chunks)
+            def _():
+                load_own(k + 2).start()
+
+        @pl.when(mid & (k >= 1) & (k < chunks + 1))
+        def _():
+            j = k - 1
+            swap(j).wait()
+            far_in[slot(j)] = near_in[slot(j)] + far_in[slot(j)]
+            send_sum(j).start()
+            emit(j, far_in)
+
+    def load_cot(r):
+        return pltpu.make_async_copy(cot_h.at[at_tile(r, BLOCK)], cot_v.at[at_tile(r, BLOCK)], lsem.at[r])
+
+    load_ctx = pltpu.make_async_copy(ctx_h, ctx_v, lsem.at[steps])
+    load_dq = pltpu.make_async_copy(dq_h, dq_v, lsem.at[steps + 1])
+
+    sv_v[...] = sv0[...]
+    sq_v[...] = jnp.zeros_like(sq_v)
+
+    def row_phase(up_v, down_v, dense_v, qkv_v, xs, pst, xhat, n2c, actc, rstd, m1, m2, xsem):
+        ntile = ff // TILE
+        dtile = cols // TILE
+
+        def load_x(r):
+            return pltpu.make_async_copy(x_h.at[at_tile(r, BLOCK)], xs.at[lax.rem(r, 2)], xsem.at[lax.rem(r, 2)])
+
+        def load_up(j):
+            return pltpu.make_async_copy(up_h.at[:, at_tile(j, TILE)], up_v.at[:, at_tile(j, TILE)], wsem.at[2 * j])
+
+        def load_down(j):
+            return pltpu.make_async_copy(down_h.at[at_tile(j, TILE)], down_v.at[at_tile(j, TILE)], wsem.at[2 * j + 1])
+
+        load_dense = pltpu.make_async_copy(dense_h, dense_v, wsem.at[2 * ntile])
+        load_qkv = pltpu.make_async_copy(qkv_h, qkv_v, wsem.at[2 * ntile + 1])
+        load_x(0).start()
+        for j in range(ntile):
+            load_up(j).start()
+            if j == 0:
+                load_cot(0).start()
+            load_down(j).start()
+        load_ctx.start()
+        load_dense.start()
+        load_dq.start()
+        load_qkv.start()
+        for r in range(1, steps):
+            load_cot(r).start()
+        pl.semaphore_wait(bar, 3 + ndp - 1)
+
+        def put_p(r, which):
+            return pltpu.make_async_copy(pst, p_h.at[pl.ds((2 * r + which) * PER, PER)], psem)
+
+        def put_n2(r):
+            return pltpu.make_async_copy(n2c, n2_h.at[at_tile(r, BLOCK)], nsem)
+
+        @pl.loop(0, steps)
+        def _(r):
+            rds = at_tile(r, BLOCK)
+            xcur = xs.at[lax.rem(r, 2)]
+            load_x(r).wait()
+            load_cot(r).wait()
+
+            @pl.when(r + 1 < steps)
+            def _():
+                load_x(r + 1).start()
+
+            @pl.when(r > 0)
+            def _():
+                put_n2(r - 1).wait()
+
+            @pl.loop(0, BLOCK // CH)
+            def _(s):
+                sds = at_tile(s, CH)
+                xf = xcur[sds, :].astype(F32)
+                centre = xf - jnp.mean(xf, axis=-1, keepdims=True)
+                inv = lax.rsqrt(jnp.mean(centre * centre, axis=-1, keepdims=True) + EPSILON)
+                xh = centre * inv
+                xhat[sds, :] = xh
+                rstd[sds, :] = jnp.broadcast_to(inv, (CH, 128))
+                n2c[sds, :] = (xh * vec[V_GAIN2 : V_GAIN2 + 1, :] + vec[V_BIAS2 : V_BIAS2 + 1, :]).astype(LOW)
+
+            put_n2(r).start()
+
+            @pl.loop(0, ntile)
+            def _(j):
+                jds = at_tile(j, TILE)
+
+                @pl.when(r == 0)
+                def _():
+                    load_up(j).wait()
+                    load_down(j).wait()
+
+                hidden = dot_nn(n2c[...], up_v[:, jds]) + vec[V_UP : V_UP + 1, jds]
+                cum = 0.5 * (1.0 + lax.erf(hidden * RSQRT2))
+                active = hidden * cum
+                slope = cum + hidden * jnp.exp(-0.5 * hidden * hidden) * RSQRT2PI
+                act_low = active.astype(LOW)
+                actc[:, jds] = act_low
+                a_t[jds, rds] = act_low.T
+                sq_v[...] += jnp.sum((active * active).reshape(BLOCK // 8, 8, TILE), axis=0)
+                d_hid = (dot_nt(cot_v[rds, :], down_v[jds, :]) * slope).astype(LOW)
+                dh_v[rds, jds] = d_hid
+                sv_v[S_UP : S_UP + 1, jds] += jnp.sum(d_hid.astype(F32), axis=0, keepdims=True)
+
+            @pl.when(r > 0)
+            def _():
+                tick(3 * r - 2)
+                put_p(r - 1, 1).wait()
+
+            @pl.when(r == 0)
+            def _():
+                load_ctx.wait()
+                load_dense.wait()
+
+            a_t[pl.ds(ff, att), rds] = ctx_v[rds, :].T
+
+            @pl.loop(0, dtile)
+            def _(j):
+                jds = at_tile(j, TILE)
+                cot_tile = cot_v[rds, jds].astype(F32)
+                sv_v[S_OUT : S_OUT + 1, jds] += jnp.sum(cot_tile, axis=0, keepdims=True)
+                term = dot_nn(actc[...], down_v[:, jds]) + dot_nn(ctx_v[rds, :], dense_v[:, jds])
+                term = term + add_here * (xcur[:, jds].astype(F32) + vec[V_OUT : V_OUT + 1, jds])
+                pst[:, :, jds] = term.reshape(PER, CH, TILE)
+
+            put_p(r, 0).start()
+
+            @pl.when(r == 0)
+            def _():
+                load_dq.wait()
+                load_qkv.wait()
+
+            put_p(r, 0).wait()
+
+            @pl.when(r == 0)
+            def _():
+                prime()
+
+            @pl.when(r > 0)
+            def _():
+                tick(3 * r - 1)
+
+            m1[...] = jnp.zeros_like(m1)
+            m2[...] = jnp.zeros_like(m2)
+            sv_v[S_QKV : S_QKV + 1, pl.ds(0, qw)] += jnp.sum(dq_v[rds, :].astype(F32), axis=0, keepdims=True)
+
+            @pl.loop(0, dtile)
+            def _(j):
+                jds = at_tile(j, TILE)
+                xh = xhat[:, jds]
+                second = dot_nt(dh_v[rds, :], up_v[jds, :])
+                sv_v[S_GAIN2 : S_GAIN2 + 1, jds] += jnp.sum(second * xh, axis=0, keepdims=True)
+                sv_v[S_BIAS2 : S_BIAS2 + 1, jds] += jnp.sum(second, axis=0, keepdims=True)
+                first = dot_nt(dq_v[rds, :], qkv_v[jds, :])
+                sv_v[S_GAIN1 : S_GAIN1 + 1, jds] += jnp.sum(first * xh, axis=0, keepdims=True)
+                sv_v[S_BIAS1 : S_BIAS1 + 1, jds] += jnp.sum(first, axis=0, keepdims=True)
+                scaled = second * vec[V_GAIN2 : V_GAIN2 + 1, jds] + first * vec[V_GAIN1 : V_GAIN1 + 1, jds]
+                pst[:, :, jds] = scaled.reshape(PER, CH, TILE)
+                with_xh = scaled * xh
+                for q in range(TILE // 128):
+                    m1[...] += scaled[:, q * 128 : (q + 1) * 128]
+                    m2[...] += with_xh[:, q * 128 : (q + 1) * 128]
+
+            @pl.loop(0, PER)
+            def _(s):
+                sds = at_tile(s, CH)
+                mean1 = jnp.sum(m1[sds, :], axis=-1, keepdims=True) * (1.0 / cols)
+                mean2 = jnp.sum(m2[sds, :], axis=-1, keepdims=True) * (1.0 / cols)
+                grad = rstd[sds, 0:1] * (pst[s] - mean1 - xhat[sds, :] * mean2)
+                cot_rows = cot_v[pl.ds(pl.multiple_of(r * BLOCK + s * CH, CH), CH), :].astype(F32)
+                pst[s] = grad + add_here * cot_rows
+
+            put_p(r, 1).start()
+            tick(3 * r)
+
+        put_p(steps - 1, 1).wait()
+        put_n2(steps - 1).wait()
+
+    pl.run_scoped(
+        row_phase,
+        pltpu.VMEM((cols, ff), LOW), pltpu.VMEM((ff, cols), LOW), pltpu.VMEM((att, cols), LOW), pltpu.VMEM((cols, qw), LOW),
+        pltpu.VMEM((2, BLOCK, cols), LOW), pltpu.VMEM((PER, CH, cols), F32), pltpu.VMEM((BLOCK, cols), F32),
+        pltpu.VMEM((BLOCK, cols), LOW), pltpu.VMEM((BLOCK, ff), LOW), pltpu.VMEM((BLOCK, 128), F32),
+        pltpu.VMEM((BLOCK, 128), F32), pltpu.VMEM((BLOCK, 128), F32), pltpu.SemaphoreType.DMA((2,)),
+    )
+    done = 3 * (steps - 1) + 1
+
+    sv_v[S_STATS : S_STATS + 1, :] += jnp.sum(sq_v[...]) * vec[V_PICK : V_PICK + 1, :]
+    svd[d] = sv_v[...]
+
+    def give_dp(k):
+        return pltpu.make_async_remote_copy(
+            src_ref=sv_v, dst_ref=svd.at[d], send_sem=ssv.at[k], recv_sem=rsv.at[d],
+            device_id=(lax.rem(d + k, ndp), t), device_id_type=MESH)
+
+    def get_dp(k):
+        other = lax.rem(d + k, ndp)
+        return pltpu.make_async_remote_copy(
+            src_ref=sv_v, dst_ref=svd.at[other], send_sem=ssv.at[k], recv_sem=rsv.at[other],
+            device_id=(other, t), device_id_type=MESH)
+
+    @pl.loop(1, ndp)
+    def _(k):
+        give_dp(k).start()
+
+    def grad_phase(n1_v, n2_v, sd, su, gsem):
+        load_n1 = pltpu.make_async_copy(n1_h, n1_v, gsem.at[0])
+        load_n2 = pltpu.make_async_copy(n2_h, n2_v, gsem.at[1])
+        load_n1.start()
+        load_n2.start()
+
+        def lanes(ref, e):
+            if width % 128 == 0:
+                return ref[:, at_tile(e, width)]
+            pair = ref[:, at_tile(lax.div(e, 2), 2 * width)]
+            odd = lax.rem(e, 2) == 1
+            return jnp.where(odd, pair[:, width:].astype(F32), pair[:, :width].astype(F32)).astype(LOW)
+
+        def give_d(i):
+            return pltpu.make_async_remote_copy(
+                src_ref=sd.at[0], dst_ref=ad_h.at[i], send_sem=sa.at[0], recv_sem=ra.at[i],
+                device_id=(mate, t), device_id_type=MESH)
+
+        def give_u(i):
+            return pltpu.make_async_remote_copy(
+                src_ref=su.at[0], dst_ref=au_h.at[i], send_sem=sa.at[1], recv_sem=ra.at[half + i],
+                device_id=(mate, t), device_id_type=MESH)
+
+        def slice_d(e, into, add):
+            right = lanes(cot_v, e)
+
+            @pl.loop(0, (ff + att) // TILE)
+            def _(j):
+                part = dot_nn(a_t[at_tile(j, TILE), :], right)
+                if add:
+                    part = part + into[at_tile(j, TILE), :]
+                into[at_tile(j, TILE), :] = part
+
+        def slice_u(e, into, add):
+            left = lanes(n2_v, e).T
+
+            @pl.loop(0, ff // TILE)
+            def _(j):
+                part = dot_nn(left, dh_v[:, at_tile(j, TILE)])
+                if add:
+                    part = part + into[:, at_tile(j, TILE)]
+                into[:, at_tile(j, TILE)] = part
+
+            left1 = lanes(n1_v, e).T
+
+            @pl.loop(0, qw // TILE)
+            def _(j):
+                part = dot_nn(left1, dq_v[:, at_tile(j, TILE)])
+                there = pl.ds(pl.multiple_of(ff + j * TILE, TILE), TILE)
+                if add:
+                    part = part + into[:, there]
+                into[:, there] = part
+
+        def own_slice(i, into, got, keep, out, first, compute):
+            e = 2 * i + parity
+            fetch = pltpu.make_async_copy(got.at[i], into, ssem)
+            fetch.start()
+            fetch.wait()
+            compute(e, into, True)
+            put = pltpu.make_async_copy(into, keep.at[i], ssem)
+            put.start()
+            put.wait()
+
+            @pl.when(e == d)
+            def _():
+                stay = pltpu.make_async_copy(into, out.at[here], ssem)
+                stay.start()
+                stay.wait()
+
+            @pl.when(e != d)
+            def _():
+                pltpu.make_async_remote_copy(
+                    src_ref=keep.at[i], dst_ref=out.at[here], send_sem=sb.at[first + i],
+                    recv_sem=rb.at[first + here], device_id=(e, t), device_id_type=MESH).start()
+
+        @pl.loop(0, half + 1)
+        def _(i):
+            base = done + 3 * i
+
+            @pl.when(i < half)
+            def _():
+                e = 2 * i + 1 - parity
+
+                @pl.when(i > 0)
+                def _():
+                    give_d(i - 1).wait_send()
+
+                slice_d(e, sd.at[0], False)
+                give_d(i).start()
+
+            tick(base)
+
+            @pl.when(i == 0)
+            def _():
+                load_n1.wait()
+                load_n2.wait()
+
+            @pl.when(i < half)
+            def _():
+                e = 2 * i + 1 - parity
+
+                @pl.when(i > 0)
+                def _():
+                    give_u(i - 1).wait_send()
+
+                slice_u(e, su.at[0], False)
+                give_u(i).start()
+
+            tick(base + 1)
+
+            @pl.when(i > 0)
+            def _():
+                give_d(i - 1).wait_recv()
+                own_slice(i - 1, sd.at[1], ad_h, bd_h, gd_h, 0, slice_d)
+                give_u(i - 1).wait_recv()
+                own_slice(i - 1, su.at[1], au_h, bu_h, gu_h, half, slice_u)
+
+            tick(base + 2)
+
+        give_d(half - 1).wait_send()
+        give_u(half - 1).wait_send()
+
+    pl.run_scoped(
+        grad_phase,
+        pltpu.VMEM((rows, cols), LOW), pltpu.VMEM((rows, cols), LOW),
+        pltpu.VMEM((2, ff + att, width), F32), pltpu.VMEM((2, width, ff + qw), F32), pltpu.SemaphoreType.DMA((2,)),
+    )
+    done2 = done + 3 * (half + 1)
+
+    @pl.loop(1, ndp)
+    def _(k):
+        get_dp(k).wait_recv()
+        give_dp(k).wait_send()
+
+    total = svd[0]
+    for i in range(1, ndp):
+        total = total + svd[i]
+    sv_o[0] = total
+    svz[t] = total
+
+    def give_z(k):
+        return pltpu.make_async_remote_copy(
+            src_ref=sv_o.at[0], dst_ref=svz.at[t], send_sem=ssz.at[k], recv_sem=rsz.at[t],
+            device_id=(d, lax.rem(t + k, 4)), device_id_type=MESH)
+
+    def get_z(k):
+        other = lax.rem(t + k, 4)
+        return pltpu.make_async_remote_copy(
+            src_ref=sv_o.at[0], dst_ref=svz.at[other], send_sem=ssz.at[k], recv_sem=rsz.at[other],
+            device_id=(d, other), device_id_type=MESH)
+
+    for k in range(1, 4):
+        give_z(k).start()
+
+    @pl.loop(done2, chunks + LAG)
+    def _(k):
+        tick(k)
+
+    for k in range(1, 4):
+        get_z(k).wait_recv()
+        give_z(k).wait_send()
+    sv_o[1] = svz[0] + svz[1] + svz[2] + svz[3]
+
+    @pl.when(mid)
+    def _():
+        @pl.loop(chunks - HELD, chunks)
+        def _(k):
+            send_sum(k).wait_send()
+
+    store(chunks - 2).wait()
+    store(chunks - 1).wait()
+
+    @pl.loop(0, half)
+    def _(i):
+        @pl.when(i != here)
+        def _():
+            for keep, out, first in ((bd_h, gd_h, 0), (bu_h, gu_h, half)):
+                sent = pltpu.make_async_remote_copy(
+                    src_ref=keep.at[i], dst_ref=out.at[i], send_sem=sb.at[first + i],
+                    recv_sem=rb.at[first + i], device_id=(2 * i + parity, t), device_id_type=MESH)
+                sent.wait_send()
+                sent.wait_recv()
+
+
+def layer(ndp, vec, sv0, x, cot, n1, ctx, dq, up_w, down_w, dense_w, qkv_w):
+    rows, cols = x.shape
+    ff, att, qw = up_w.shape[1], ctx.shape[1], dq.shape[1]
+    width, half, steps, chunks = cols // ndp, ndp // 2, rows // BLOCK, 2 * rows // CH
+    any_spec = pl.BlockSpec(memory_space=pl.ANY)
+    vmem_spec = pl.BlockSpec(memory_space=pltpu.VMEM)
+    sem = pltpu.SemaphoreType.DMA
+    return pl.pallas_call(
+        functools.partial(layer_kernel, ndp),
+        out_shape=[
+            jax.ShapeDtypeStruct((chunks, CH, cols), LOW),
+            jax.ShapeDtypeStruct((2, SV, cols), F32),
+            jax.ShapeDtypeStruct((half, ff + att, width), F32),
+            jax.ShapeDtypeStruct((half, width, ff + qw), F32),
+            jax.ShapeDtypeStruct((chunks, CH, cols), F32),
+            jax.ShapeDtypeStruct((rows, cols), LOW),
+            jax.ShapeDtypeStruct((half, ff + att, width), F32),
+            jax.ShapeDtypeStruct((half, width, ff + qw), F32),
+            jax.ShapeDtypeStruct((half, ff + att, width), F32),
+            jax.ShapeDtypeStruct((half, width, ff + qw), F32),
+        ],
+        in_specs=[vmem_spec, vmem_spec] + [any_spec] * 9,
+        out_specs=[any_spec, vmem_spec] + [any_spec] * 8,
+        scratch_shapes=[
+            pltpu.VMEM((ff + att, rows), LOW), pltpu.VMEM((rows, cols), LOW), pltpu.VMEM((rows, ff), LOW),
+            pltpu.VMEM((rows, qw), LOW), pltpu.VMEM((rows, att), LOW), pltpu.VMEM((SV, cols), F32),
+            pltpu.VMEM((8, TILE), F32), pltpu.VMEM((ndp, SV, cols), F32), pltpu.VMEM((4, SV, cols), F32),
+            pltpu.VMEM((WINDOW, CH, cols), F32), pltpu.VMEM((WINDOW, CH, cols), F32),
+            pltpu.VMEM((2, CH, cols), F32), pltpu.VMEM((2, CH, cols), LOW),
+            sem((WINDOW,)), sem((WINDOW,)), sem((WINDOW,)), sem((WINDOW,)), sem((2,)), sem((2,)),
+            sem((steps + 2,)), sem((2 * (ff // TILE) + 2,)), sem, sem,
+            sem((ndp,)), sem((ndp,)), sem((4,)), sem((4,)),
+            sem((2,)), sem((2 * half,)), sem((2 * half,)), sem((2 * half,)), sem,
+        ],
+        compiler_params=pltpu.CompilerParams(
+            collective_id=0, has_side_effects=True, vmem_limit_bytes=VMEM_ASK),
+        cost_estimate=pl.CostEstimate(flops=10**11, bytes_accessed=2 * 10**8, transcendentals=0),
+        name="layer",
+    )(vec, sv0, x, cot, n1, ctx, dq, up_w, down_w, dense_w, qkv_w)
 
 
 def layer_norm(resid, norm_gain, norm_bias):
@@ -67,6 +635,7 @@
 
 
 def on_device(
+    ndp,
     inputs,
     cotangent,
     segments,
@@ -125,33 +694,7 @@
 
     context, log_totals = lax.map(attend, (queries, key_rows, values, segments))
     context_low = context.reshape(rows_here, heads_here * HS).astype(jnp.bfloat16)
-    attn_part = jnp.dot(context_low, dense_weight, preferred_element_type=jnp.float32)
-    second_full, pull_second = jax.vjp(layer_norm, resid, ln2_gain, ln2_bias)
-    second_norm = second_full.astype(jnp.bfloat16)
-    hidden = jnp.dot(second_norm, up_weight, preferred_element_type=jnp.float32) + up_bias
-    active, pull_active = jax.vjp(gelu_exact, hidden)
-    active_low = active.astype(jnp.bfloat16)
-    branch_terms = attn_part + jnp.dot(active_low, down_weight, preferred_element_type=jnp.float32)
-    branches = lax.psum(branch_terms, "tensor")
-    out = (resid + branches + dense_bias + down_bias).astype(jnp.bfloat16)
-    context_seq = jnp.sum((context * context).reshape(seqs_here, -1), axis=1)
-    active_seq = jnp.sum((active * active).reshape(seqs_here, -1), axis=1)
-    count_seq = jnp.where(lax.axis_index("tensor") == 0, float(LEN), 0.0) * jnp.ones_like(
-        context_seq
-    )
-    subset_pick = (subsets[:, None] == jnp.arange(SUBSETS)[None, :]).astype(jnp.float32)
-    per_seq = jnp.stack([context_seq, active_seq, count_seq], axis=1)
-    stats_local = jnp.sum(subset_pick[:, :, None] * per_seq[:, None, :], axis=0)
-    stats_total = lax.psum(stats_local, ("dp", "tensor"))
-    grad_full = cotangent.astype(jnp.float32)
-    out_bias_grad = jnp.sum(grad_full, axis=0)
-    down_grad = dot_rows(active_low, cotangent)
-    dense_grad = dot_rows(context_low, cotangent)
-    d_active = dot_cols(cotangent, down_weight)
-    d_hidden = pull_active(d_active)[0].astype(jnp.bfloat16)
-    up_bias_grad = jnp.sum(d_hidden, axis=0, dtype=jnp.float32)
-    d_second = dot_cols(d_hidden, up_weight)
-    dx_second, dgain_second, dbias_second = pull_second(d_second)
+    context_sq = jnp.sum(context * context)
     d_context = dot_cols(cotangent, dense_weight).astype(jnp.bfloat16)
     d_context = d_context.reshape(seqs_here, LEN, heads_here, HS)
 
@@ -194,38 +737,46 @@
     )
     d_joined = jnp.stack([pull_turn(query_grad)[0], pull_turn(key_grad)[0], value_grad], axis=3)
     d_joined = d_joined.reshape(rows_here, 3 * heads_here * HS).astype(jnp.bfloat16)
-    qkv_bias_grad = jnp.sum(d_joined, axis=0, dtype=jnp.float32)
-    d_first = dot_cols(d_joined, qkv_weight)
-    dx_first, dgain_first, dbias_first = pull_first(d_first)
-    qkv_part, dense_part, up_part, down_part = (
-        lax.psum_scatter(dot_rows(first_norm, d_joined), "dp", scatter_dimension=0, tiled=True),
-        lax.psum_scatter(dense_grad, "dp", scatter_dimension=1, tiled=True),
-        lax.psum_scatter(dot_rows(second_norm, d_hidden), "dp", scatter_dimension=0, tiled=True),
-        lax.psum_scatter(down_grad, "dp", scatter_dimension=1, tiled=True),
-    )
-    norm_part = jnp.stack([dgain_first, dbias_first, dgain_second, dbias_second], axis=0)
-    input_sum, norm_group = lax.psum((dx_first + dx_second, norm_part), "tensor")
-    bias_qkv, bias_up, bias_out, norm_total = lax.psum(
-        (qkv_bias_grad, up_bias_grad, out_bias_grad, norm_group), "dp"
-    )
-    input_grad = (grad_full + input_sum).astype(jnp.bfloat16)
+    model = inputs.shape[1]
+    hidden_here = up_weight.shape[1]
+    lane = jnp.arange(model)
+    slot_of = 3 * subsets[0]
+    count = jnp.where(lax.axis_index("tensor") == 0, float(LEN), 0.0)
+    stats_row = jnp.where(lane == slot_of, context_sq, 0.0) + jnp.where(lane == slot_of + 2, count, 0.0)
+    sv0 = jnp.zeros((SV, model), F32).at[S_STATS].set(stats_row)
+    pick = (lane == slot_of + 1).astype(F32)
+    blank = jnp.zeros((model,), F32)
+    up_row = jnp.pad(up_bias, (0, model - hidden_here)) if hidden_here < model else up_bias
+    vec = jnp.stack([up_row, ln1_gain, ln2_gain, ln2_bias, dense_bias + down_bias, pick, blank, blank])
+    done = layer(
+        ndp, vec, sv0, inputs, cotangent, first_norm, context_low, d_joined, up_weight, down_weight, dense_weight, qkv_weight)
+    sums, small, grads_d, grads_u = done[:4]
+    sums = sums.reshape(rows_here // BLOCK, 2, BLOCK, model)
+    out = sums[:, 0].reshape(rows_here, model)
+    input_grad = sums[:, 1].reshape(rows_here, model)
+    down_part = jnp.sum(grads_d[:, :hidden_here], axis=0)
+    dense_part = jnp.sum(grads_d[:, hidden_here:], axis=0)
+    up_part = jnp.sum(grads_u[:, :, :hidden_here], axis=0)
+    qkv_part = jnp.sum(grads_u[:, :, hidden_here:], axis=0)
+    stats_total = small[1, S_STATS, : 3 * SUBSETS].reshape(SUBSETS, 3)
     widths = jnp.array([HEADS * HS, FF], jnp.float32)
     subset_rms = jnp.sqrt(
         stats_total[:, :2] / (jnp.maximum(stats_total[:, 2:3], 1.0) * widths[None, :])
     )
+    bias_out = small[0, S_OUT]
     return (
         out,
         input_grad,
-        norm_total[0],
-        norm_total[1],
+        small[1, S_GAIN1],
+        small[1, S_BIAS1],
         qkv_part,
-        bias_qkv,
+        small[0, S_QKV, : qkv_bias.shape[0]],
         dense_part,
         bias_out,
-        norm_total[2],
-        norm_total[3],
+        small[1, S_GAIN2],
+        small[1, S_BIAS2],
         up_part,
-        bias_up,
+        small[0, S_UP, :hidden_here],
         down_part,
         bias_out,
         subset_rms,
@@ -252,7 +803,7 @@
         P(),
     )
     return jax.shard_map(
-        on_device,
+        functools.partial(on_device, mesh.shape["dp"]),
         mesh=mesh,
         in_specs=placed,
         out_specs=(

time: 842 us -> 591 us (0.70)
  Pallas kernels: 0 us -> 455 us
  waiting for transfers between devices: 435 us -> 0 us
  matrix products: 190 us -> 33.6 us
  blocking collectives: 92.4 us -> 0 us
  other arithmetic: 59.8 us -> 42.4 us
  local copies, waits for them, and re-layouts: 30.9 us -> 48.2 us
  between operations: 17.5 us -> 2.06 us
    pallas_call x0 -> x1, Pallas kernels: none -> 455 us  [layer(): pl.pallas_call(functools.partial(layer_kernel, ndp), out_shape=[jax.Shape...]
    psum x1 -> x0, waiting for transfers between devices: 435 us -> none  [on_device(): branches = lax.psum(branch_terms, 'tensor')]
    dot_general x7 -> x0, matrix products: 110 us -> none  [the longest x4 53 us: dot_rows(): lax.dot_general(left, right, (((0,), (0,)), ((), ())), preferred_element_...]
    psum x3 -> x0, blocking collectives: 92.4 us -> none  [the longest x1 48.7 us: on_device(): stats_total = lax.psum(stats_local, ('dp', 'tensor'))]
    dot_general x4 -> x1, matrix products: 50.9 us -> 5.37 us  [dot_cols(): lax.dot_general(left, right, (((1,), (1,)), ((), ())), preferred_element_...]
    slice x1 -> x4, local copies, waits for them, and re-layouts: 0.63 us -> 9.94 us  [the longest x1 6.16 us: on_device(): input_grad = sums[:, 1].reshape(rows_here, model)]
    reduce_sum x4 -> x5, other arithmetic: 23.3 us -> 18.6 us  [the longest x1 5.72 us: on_device(): down_part = jnp.sum(grads_d[:, :hidden_here], axis=0)]
  transfers between devices with their start and end apart: 5 -> 0, of which waited for: 1 -> 0; matrix products, arithmetic and copies ran while one was open for 9% -> 0% of each run, Pallas kernels for 0% -> 0%
where the time goes in v2:
time: 591 us; the launch traced here: 582 us
  Pallas kernels  455 us (77%)
  local copies, waits for them, and re-layouts  48.2 us (8%)
  other arithmetic  42.4 us (7%)
  matrix products  33.6 us (6%)
    pallas_call x1, Pallas kernels, layer(): pl.pallas_call(functools.partial(layer_kernel, ndp), out_shape=[jax.Shape...  455 us

profile of v2, /device:TPU:10, one launch (start us, length us, event | category | flops | bytes accessed | tf_op | source)
XLA Modules:
  0.0 581.7 jit_solution(13977914821550253431)
XLA Ops:
  1.4 3.0 convert_reduce_fusion
  4.4 0.4 copy-done
  4.8 1.2 fusion.2
  6.1 0.7 stack.44.vec
  7.0 2.2 fusion.41
  9.2 2.0 fusion.17
  11.2 5.4 convolution_convert_fusion
  16.6 1.1 fusion.54
  17.7 1.9 fusion.5.n1_h
  19.6 2.0 copy-done.7
  21.6 8.7 %convolution_add_fusion = f32[1024,1536]{1,0:T(8,128)} fusion(bf16[1024,2048]{1,0:T(8,128)(2,1)S(1)} %fusion.5.n1_h, bf16[2048,1536]{1,0:T(8,128)(2,1)S(1)} %bitcast.125, f32[1536]{0:T(1024)S(1)} %copy-done.22), kind=kOutput, calls=%fused_computation.11 | convolution fusion | flops 6444023808 | bytes 16783360 | tf_op jit(solution)/shard_map/dot_general | solution.py:664
  30.2 6.5 %copy.52 = f32[1024,1536]{0,1:T(8,128)} copy(f32[1024,1536]{1,0:T(8,128)} %convolution_add_fusion) | data formatting | bytes 12582912 | tf_op jit(solution)/shard_map/add | solution.py:664
  36.8 4.8 fusion.51
  41.6 1.9 copy.90
  43.5 1.3 fusion.30
  44.9 3.1 copy.89
  47.9 2.0 slice.236
  49.9 2.4 slice_negate_fusion.2
  52.3 0.7 fusion.38
  53.1 0.5 copy-done.9
  53.7 1.6 fusion.57
  55.3 1.1 fusion.7
  56.5 2.2 bitcast_convert_fusion
  58.6 1.3 fusion.10
  59.9 1.8 multiply_reduce_fusion
  61.7 0.8 multiply_convert_fusion
  62.6 0.8 fusion.26
  63.6 1.6 fusion.58
  65.3 1.1 fusion.6
  66.4 2.3 fusion.23
  68.7 2.2 bitcast_convert_fusion.1
  70.8 1.3 multiply_reduce_fusion.1
  72.2 0.8 multiply_convert_fusion.1
  73.0 0.8 fusion.27
  74.0 1.1 fusion.45
  75.2 2.5 multiply_bitcast_fusion
  77.6 1.1 pad_maximum_fusion.2
  78.7 2.4 copy.88.ctx_h
  81.2 2.7 fusion.14
  83.9 0.7 fusion.44
  84.5 0.6 scatter.4.sv0
  85.2 1.5 slice_multiply_fusion.3
  86.7 0.3 fusion.52
  87.1 0.6 split.36
  87.7 0.6 split.32
  88.3 0.3 fusion.53
  88.7 0.6 pad_add_fusion.1
  89.3 0.5 fusion.29
  89.8 0.5 fusion.28
  90.3 0.2 copy-done.8
  90.5 0.3 pad_maximum_fusion
  90.9 3.0 copy.71
  93.9 4.6 copy.72.dq_h
  98.6 455.4 %layer.1 = (bf16[64,32,2048]{2,1,0:T(8,128)(2,1)}, f32[2,8,2048]{2,1,0:T(8,128)}, f32[4,2560,256]{2,1,0:T(8,128)}, f32[4,256,3584]{2,1,0:T(8,128)}, f32[64,32,20...) custom-call(f32[8,2048]{1,0:T(8,128)} %stack.44.vec, ...), custom_call_target="tpu_custom_call" | custom-call | flops 99999997952 | bytes 200000000 | tf_op jit(solution)/shard_map/layer/pallas_call | solution.py:552
  554.0 6.2 %fusion.50 = (bf16[4,1,256,2048]{3,2,1,0:T(8,128)(2,1)}, bf16[4,1,256,2048]{3,2,1,0:T(8,128)(2,1)}) fusion(bf16[4,2,256,2048]{3,2,1,0:T(8,128)(2,1)} %bitcast.99), kind=kLoop, calls=%fused_computation.108 | loop fusion | bytes 16777216 | tf_op jit(solution)/shard_map/slice | solution.py:756
  560.1 0.7 slice_reduce_fusion.5
  560.8 1.4 slice_reduce_fusion.4
  562.2 1.7 fusion.55
  564.3 0.7 copy.73
  564.9 2.6 slice_reduce_fusion.3
  567.5 5.7 slice_reduce_fusion
  573.2 5.4 slice_reduce_fusion.2
  578.7 2.2 slice_reduce_fusion.1
  580.9 0.6 copy.101
  (67 shorter events, 1.2 us)
Async XLA Ops:
  1.3 3.5 copy-start
  1.3 4.7 copy-start.14
  1.3 4.7 copy-start.16
  1.4 4.7 copy-start.17
  1.4 4.7 copy-start.12
  1.4 4.7 copy-start.18
  1.4 4.7 copy-start.19
  1.4 4.7 copy-start.20
  9.2 12.4 %slice-start.2 = ((s8[6291456]{0:T(1024)(128)(4,1)}), s8[4194304]{0:T(1024)(128)(4,1)S(1)}, s32[]{:S(2)}) async-start(s8[6291456]{0:T(1024)(128)(4,1)} %bitcast.124), calls=%async_computation.2 | async-start | bytes 8388608
  11.2 6.5 %copy-start.1 = (bf16[1024,2048]{1,0:T(8,128)(2,1)S(1)}, bf16[1024,2048]{1,0:T(8,128)(2,1)}, u32[]{:S(2)}) copy-start(bf16[1024,2048]{1,0:T(8,128)(2,1)} %x_h.1) | copy-start | bytes 12582916
  11.2 6.5 %copy-start.15 = (f32[2048]{0:T(1024)S(1)}, f32[2048]{0:T(1024)}, u32[]{:S(2)}) copy-start(f32[2048]{0:T(1024)} %param.24) | copy-start | bytes 24580
  11.2 10.4 %slice-start.3 = ((s8[6291456]{0:T(1024)(128)(4,1)}), s8[2097152]{0:T(1024)(128)(4,1)S(1)}, s32[]{:S(2)}) async-start(s8[6291456]{0:T(1024)(128)(4,1)} %bitcast.124), calls=%async_computation.3 | async-start | bytes 4194304
  17.7 3.9 copy-start.22
  19.6 2.0 copy-start.7
  49.9 2.4 copy-start.3
  52.3 1.2 copy-start.9
  52.3 1.3 copy-start.11
  53.1 3.4 slice-start
  53.7 2.8 slice-start.1
  56.5 2.2 copy-start.6
  62.6 1.0 copy-start.10
  65.3 1.1 copy-start.5
  85.2 1.9 copy-start.2
  89.3 1.2 copy-start.8
  554.0 10.2 %copy-start.21 = (f32[2]{0:T(128)S(1)}, f32[2]{0:T(128)}, u32[]{:S(2)}) copy-start(f32[2]{0:T(128)} %constant.116.clone) | copy-start | bytes 28
  563.9 17.0 %copy-start.13 = (f32[1,1,2048]{2,1,0:T(1,128)}, f32[1,1,2048]{2,1,0:T(1,128)S(1)}, u32[]{:S(2)}) copy-start(f32[1,1,2048]{2,1,0:T(1,128)S(1)} %get-tuple-element.141) | copy-start | bytes 24580
  567.5 11.2 %copy-start.4 = (f32[4,256,3584]{2,1,0:T(8,128)S(1)}, f32[4,256,3584]{2,1,0:T(8,128)}, u32[]{:S(2)}) copy-start(f32[4,256,3584]{2,1,0:T(8,128)} %get-tuple-element.84) | copy-start | bytes 44040196

commit v3 on v0

v3 whole, which is shorter than its diff:
```python
import functools

import jax
import jax.numpy as jnp
import numpy as np
from jax import lax
from jax.experimental import pallas as pl
from jax.experimental.pallas import tpu as pltpu
from jax.sharding import PartitionSpec as P

HEADS = 8
HS = 256
ROT = 64
FF = 8192
SUBSETS = 22
LEN = 1024


EPSILON = 1e-05
MASKED_SCORE = -1000000000.0


VMEM_ASK = 64 * 2**20

MESH = pl.DeviceIdType.MESH
F32 = jnp.float32
LOW = jnp.bfloat16
BLOCK = 256
REACH = 3
CH = 32
PER = BLOCK // CH
WINDOW = 8
HELD = 4
LAG = 5
PACED = 4
TILE = 512
SUB = 16
RSQRT2 = 0.7071067811865476
RSQRT2PI = 0.3989422804014327
SV = 8
S_GAIN1, S_BIAS1, S_GAIN2, S_BIAS2, S_STATS, S_UP, S_QKV, S_OUT = range(SV)
VROWS = 16
V_UP, V_GAIN1, V_BIAS1, V_GAIN2, V_BIAS2, V_OUT, V_QKV, V_CTX, V_ACT, V_COUNT = range(10)


def dot_nn(left, right):
    return lax.dot_general(left, right, (((1,), (0,)), ((), ())), preferred_element_type=F32)


def dot_nt(left, right):
    return lax.dot_general(left, right, (((1,), (1,)), ((), ())), preferred_element_type=F32)


def at_tile(index, width):
    return pl.ds(pl.multiple_of(index * width, width), width)


def turn_tables(packed):
    lane = lax.broadcasted_iota(jnp.int32, packed.shape, 1)
    half_rot = ROT // 2
    sine = pltpu.roll(packed, 64, 1)
    cosine = jnp.where(lane < ROT, packed, 1.0)
    from_upper = jnp.where(lane < half_rot, -sine, 0.0)
    from_lower = jnp.where((lane >= half_rot) & (lane < ROT), sine, 0.0)
    return cosine, from_upper, from_lower


def turn(head, tables, sign):
    cosine, from_upper, from_lower = tables
    low_part = head[:, :128]
    moved = pltpu.roll(low_part, 128 - ROT // 2, 1) * from_upper + pltpu.roll(low_part, ROT // 2, 1) * from_lower
    low_part = low_part * cosine + moved if sign > 0 else low_part * cosine - moved
    return jnp.concatenate([low_part, head[:, 128:]], axis=1)


def layer_kernel(
    ndp,
    vec, seg, x_h, cot_h, rot_h, up_h, down_h, dense_h, qkv_h,
    o_h, sv_o, gd_h, gu_h, gq_h, p_h, n1_h, n2_h, ad_h, au_h, aq_h, bd_h, bu_h, bq_h,
    a_t, cot_v, dh_v, dq_v, q_v, k_v, v_v, do_v, lse_v, rot_v, sv_v, sq_v, csq_v, svd, svz,
    near_in, far_in, own, low,
    s1, r1, s2, r2, lp, lo, lsem, wsem, psem, nsem,
    ssv, rsv, ssz, rsz, sa, ra, sb, rb, ssem,
):
    d = lax.axis_index("dp")
    t = lax.axis_index("tensor")
    rows, cols = x_h.shape
    ff = up_h.shape[1]
    att = dense_h.shape[0]
    heads = att // HS
    qw = qkv_h.shape[1]
    width = cols // ndp
    half = ndp // 2
    steps = rows // BLOCK
    chunks = 2 * rows // CH
    near = t + 1 - 2 * lax.rem(t, 2)
    far = 3 - t
    mid = (t == 1) | (t == 2)
    end = jnp.logical_not(mid)
    parity = lax.rem(d, 2)
    mate = d + 1 - 2 * parity
    here = lax.div(d, 2)
    add_here = jnp.where(t == 1, 1.0, 0.0).astype(F32)

    bar = pltpu.get_barrier_semaphore()
    for k in range(1, 4):
        pl.semaphore_signal(bar, inc=1, device_id=(d, lax.rem(t + k, 4)), device_id_type=MESH)

    @pl.loop(1, ndp)
    def _(k):
        pl.semaphore_signal(bar, inc=1, device_id=(lax.rem(d + k, ndp), t), device_id_type=MESH)

    def slot(k):
        return lax.rem(k, WINDOW)

    def send_part(k):
        return pltpu.make_async_remote_copy(
            src_ref=p_h.at[k], dst_ref=near_in.at[slot(k)], send_sem=s1.at[slot(k)],
            recv_sem=r1.at[slot(k)], device_id=(d, near), device_id_type=MESH)

    def swap(k):
        return pltpu.make_async_remote_copy(
            src_ref=near_in.at[slot(k)], dst_ref=far_in.at[slot(k)], send_sem=s2.at[slot(k)],
            recv_sem=r2.at[slot(k)], device_id=(d, far), device_id_type=MESH)

    def send_sum(k):
        return pltpu.make_async_remote_copy(
            src_ref=far_in.at[slot(k)], dst_ref=near_in.at[slot(k)], send_sem=s1.at[slot(k)],
            recv_sem=r1.at[slot(k)], device_id=(d, near), device_id_type=MESH)

    def load_own(k):
        return pltpu.make_async_copy(p_h.at[k], own.at[lax.rem(k, 2)], lp.at[lax.rem(k, 2)])

    def store(k):
        return pltpu.make_async_copy(low.at[lax.rem(k, 2)], o_h.at[k], lo.at[lax.rem(k, 2)])

    def emit(k, ref):
        @pl.when(k >= 2)
        def _():
            store(k - 2).wait()

        low[lax.rem(k, 2)] = ref[slot(k)].astype(LOW)
        store(k).start()

    def prime():
        @pl.when(end)
        def _():
            @pl.loop(0, WINDOW)
            def _(k):
                send_part(k).start()

        @pl.when(mid)
        def _():
            load_own(0).start()
            load_own(1).start()

    def tick(k):
        @pl.when(end & (k >= LAG) & (k < chunks + LAG))
        def _():
            j = k - LAG
            send_sum(j).wait_recv()
            send_part(j).wait_send()
            emit(j, near_in)

            @pl.when(j + WINDOW < chunks)
            def _():
                send_part(j + WINDOW).start()

        @pl.when(mid & (k < chunks))
        def _():
            send_part(k).wait_recv()
            load_own(k).wait()
            near_in[slot(k)] = near_in[slot(k)] + own[lax.rem(k, 2)]

            @pl.when(k >= HELD)
            def _():
                send_sum(k - HELD).wait_send()

            swap(k).start()

            @pl.when(k + 2 < chunks)
            def _():
                load_own(k + 2).start()

        @pl.when(mid & (k >= 1) & (k < chunks + 1))
        def _():
            j = k - 1
            swap(j).wait()
            far_in[slot(j)] = near_in[slot(j)] + far_in[slot(j)]
            send_sum(j).start()
            emit(j, far_in)

    ntile, dtile = ff // TILE, cols // TILE

    def load_cot(r):
        return pltpu.make_async_copy(cot_h.at[at_tile(r, BLOCK)], cot_v.at[at_tile(r, BLOCK)], lsem.at[r])

    def load_x(r, xs, xsem):
        return pltpu.make_async_copy(x_h.at[at_tile(r, BLOCK)], xs.at[lax.rem(r, 2)], xsem.at[lax.rem(r, 2)])

    def put_p(r, which, pst):
        first = pl.multiple_of(which * (chunks // 2) + r * PER, PER)
        return pltpu.make_async_copy(pst, p_h.at[pl.ds(first, PER)], psem)

    def seen(r):
        return pl.ds(pl.multiple_of(jnp.maximum(r - (REACH - 1), 0) * BLOCK, BLOCK), REACH * BLOCK)

    def allowed(r):
        keys = REACH * BLOCK
        first = jnp.maximum(r - (REACH - 1), 0) * BLOCK
        query_at = lax.broadcasted_iota(jnp.int32, (BLOCK, keys), 0) + r * BLOCK
        key_at = lax.broadcasted_iota(jnp.int32, (BLOCK, keys), 1) + first
        query_seg = jnp.broadcast_to(seg[0:1, at_tile(r, BLOCK)], (8, BLOCK)).T[:, 0:1]
        return (query_seg == seg[0:1, seen(r)]) & (key_at <= query_at)

    sv_v[...] = jnp.zeros_like(sv_v)
    sq_v[...] = jnp.zeros_like(sq_v)
    csq_v[...] = jnp.zeros_like(csq_v)
    score_scale = HS ** (-0.5)

    def with_inputs(up_v, qkv_v):
        def load_up(j):
            return pltpu.make_async_copy(up_h.at[:, at_tile(j, TILE)], up_v.at[:, at_tile(j, TILE)], wsem.at[2 * j])

        load_qkv = pltpu.make_async_copy(qkv_h, qkv_v, wsem.at[2 * ntile + 1])
        load_rot = pltpu.make_async_copy(rot_h, rot_v, lsem.at[steps])

        def forward_phase(down_v, dense_v, xs, pst, n1c, n2c, actc, slope, ctxc, xsem):
            def load_down(j):
                return pltpu.make_async_copy(down_h.at[at_tile(j, TILE)], down_v.at[at_tile(j, TILE)], wsem.at[2 * j + 1])

            load_dense = pltpu.make_async_copy(dense_h, dense_v, wsem.at[2 * ntile])
            load_x(0, xs, xsem).start()
            load_qkv.start()
            load_rot.start()
            load_cot(0).start()
            load_dense.start()
            for j in range(ntile):
                load_up(j).start()
            for j in range(ntile):
                load_down(j).start()
            for r in range(1, steps):
                load_cot(r).start()
            k_v[...] = jnp.zeros_like(k_v)
            v_v[...] = jnp.zeros_like(v_v)
            pl.semaphore_wait(bar, 3 + ndp - 1)

            def put_n(r):
                return (
                    pltpu.make_async_copy(n1c, n1_h.at[at_tile(r, BLOCK)], nsem.at[0]),
                    pltpu.make_async_copy(n2c, n2_h.at[at_tile(r, BLOCK)], nsem.at[1]),
                )

            @pl.loop(0, steps)
            def _(r):
                rds = at_tile(r, BLOCK)
                xcur = xs.at[lax.rem(r, 2)]
                load_x(r, xs, xsem).wait()

                @pl.when(r + 1 < steps)
                def _():
                    load_x(r + 1, xs, xsem).start()

                @pl.when(r > 0)
                def _():
                    for copy in put_n(r - 1):
                        copy.wait()

                @pl.loop(0, BLOCK // SUB, unroll=2)
                def _(s):
                    sds = at_tile(s, SUB)
                    xf = xcur[sds, :].astype(F32)
                    centre = xf - jnp.mean(xf, axis=-1, keepdims=True)
                    xh = centre * lax.rsqrt(jnp.mean(centre * centre, axis=-1, keepdims=True) + EPSILON)
                    n1c[sds, :] = (xh * vec[V_GAIN1 : V_GAIN1 + 1, :] + vec[V_BIAS1 : V_BIAS1 + 1, :]).astype(LOW)
                    n2c[sds, :] = (xh * vec[V_GAIN2 : V_GAIN2 + 1, :] + vec[V_BIAS2 : V_BIAS2 + 1, :]).astype(LOW)

                for copy in put_n(r):
                    copy.start()

                @pl.when(r == 0)
                def _():
                    load_qkv.wait()
                    load_rot.wait()

                tables = turn_tables(rot_v[rds, :])
                for h in range(heads):
                    for part in range(3):
                        at = pl.ds((3 * h + part) * HS, HS)
                        head = dot_nn(n1c[...], qkv_v[:, at]) + vec[V_QKV : V_QKV + 1, at]
                        if part < 2:
                            head = turn(head, tables, 1)
                        (q_v, k_v, v_v)[part][h, rds, :] = head.astype(LOW)

                load_cot(r).wait()

                @pl.when(r == 0)
                def _():
                    load_dense.wait()

                do_v[rds, :] = dot_nt(cot_v[rds, :], dense_v[...]).astype(LOW)

                ok = allowed(r)
                for h in range(heads):
                    scores = dot_nt(q_v[h, rds, :], k_v[h, seen(r), :]) * score_scale
                    scores = jnp.where(ok, scores, MASKED_SCORE)
                    peak = jnp.max(scores, axis=-1, keepdims=True)
                    weights = jnp.exp(scores - peak)
                    total = jnp.sum(weights, axis=-1, keepdims=True)
                    lse_v[rds, h * 64 : h * 64 + 64] = jnp.broadcast_to(peak + jnp.log(total), (BLOCK, 64))
                    context = dot_nn((weights / total).astype(LOW), v_v[h, seen(r), :])
                    csq_v[...] += jnp.sum((context * context).reshape(BLOCK // 8, 8, HS), axis=0)
                    context = context.astype(LOW)
                    ctxc[:, h * HS : (h + 1) * HS] = context
                    a_t[pl.ds(ff + h * HS, HS), rds] = context.T

                @pl.when(r > 0)
                def _():
                    tick(4 * r - 3)

                @pl.loop(0, ntile)
                def _(j):
                    jds = at_tile(j, TILE)

                    @pl.when(r == 0)
                    def _():
                        load_up(j).wait()

                    hidden = dot_nn(n2c[...], up_v[:, jds]) + vec[V_UP : V_UP + 1, jds]
                    cum = 0.5 * (1.0 + lax.erf(hidden * RSQRT2))
                    active = hidden * cum
                    slope[:, jds] = cum + hidden * jnp.exp(-0.5 * hidden * hidden) * RSQRT2PI
                    act_low = active.astype(LOW)
                    actc[:, jds] = act_low
                    sq_v[...] += jnp.sum((active * active).reshape(BLOCK // 8, 8, TILE), axis=0)

                @pl.when(r > 0)
                def _():
                    tick(4 * r - 2)

                @pl.when(r == 0)
                def _():
                    @pl.loop(0, ntile)
                    def _(j):
                        load_down(j).wait()

                @pl.loop(0, dtile)
                def _(j):
                    jds = at_tile(j, TILE)
                    term = dot_nn(actc[...], down_v[:, jds]) + dot_nn(ctxc[...], dense_v[:, jds])
                    term = term + add_here * (xcur[:, jds].astype(F32) + vec[V_OUT : V_OUT + 1, jds])
                    pst[:, :, jds] = term.reshape(PER, CH, TILE)

                put_p(r, 0, pst).start()

                @pl.loop(0, ntile)
                def _(j):
                    jds = at_tile(j, TILE)
                    a_t[jds, rds] = actc[:, jds].T

                put_p(r, 0, pst).wait()

                @pl.when(r == 0)
                def _():
                    prime()

                @pl.when(r > 0)
                def _():
                    tick(4 * r - 1)

                @pl.loop(0, ntile)
                def _(j):
                    jds = at_tile(j, TILE)
                    d_hid = (dot_nt(cot_v[rds, :], down_v[jds, :]) * slope[:, jds]).astype(LOW)
                    dh_v[rds, jds] = d_hid
                    sv_v[S_UP : S_UP + 1, jds] += jnp.sum(d_hid.astype(F32), axis=0, keepdims=True)

                tick(4 * r)

            for copy in put_n(steps - 1):
                copy.wait()

        pl.run_scoped(
            forward_phase,
            pltpu.VMEM((ff, cols), LOW), pltpu.VMEM((att, cols), LOW),
            pltpu.VMEM((2, BLOCK, cols), LOW), pltpu.VMEM((PER, CH, cols), F32),
            pltpu.VMEM((BLOCK, cols), LOW), pltpu.VMEM((BLOCK, cols), LOW), pltpu.VMEM((BLOCK, ff), LOW),
            pltpu.VMEM((BLOCK, ff), F32), pltpu.VMEM((BLOCK, att), LOW), pltpu.SemaphoreType.DMA((2,)),
        )
        done = 4 * (steps - 1) + 1

        def lanes(ref, e):
            if width % 128 == 0:
                return ref[:, at_tile(e, width)]
            pair = ref[:, at_tile(lax.div(e, 2), 2 * width)]
            odd = lax.rem(e, 2) == 1
            return jnp.where(odd, pair[:, width:].astype(F32), pair[:, :width].astype(F32)).astype(LOW)

        def by_rows(right_ref):
            def compute(e, into, add):
                right = lanes(right_ref, e)

                @pl.loop(0, (ff + att) // TILE)
                def _(j):
                    part = dot_nn(a_t[at_tile(j, TILE), :], right)
                    if add:
                        part = part + into[at_tile(j, TILE), :]
                    into[at_tile(j, TILE), :] = part

            return compute

        def by_columns(left_ref, right_ref):
            def compute(e, into, add):
                left = lanes(left_ref, e).T

                @pl.loop(0, right_ref.shape[1] // TILE)
                def _(j):
                    part = dot_nn(left, right_ref[:, at_tile(j, TILE)])
                    if add:
                        part = part + into[:, at_tile(j, TILE)]
                    into[:, at_tile(j, TILE)] = part

            return compute

        def give(group, i, buf, got):
            return pltpu.make_async_remote_copy(
                src_ref=buf.at[0], dst_ref=got.at[i], send_sem=sa.at[group], recv_sem=ra.at[group * half + i],
                device_id=(mate, t), device_id_type=MESH)

        def mate_slice(group, i, buf, got, compute, again):
            @pl.when(again)
            def _():
                give(group, i, buf, got).wait_send()

            compute(2 * i + 1 - parity, buf.at[0], False)
            give(group, i, buf, got).start()

        def fetch(group, i, buf, got):
            return pltpu.make_async_copy(got.at[i], buf.at[1], ssem.at[group])

        def get_slice(group, i, buf, got):
            give(group, i, buf, got).wait_recv()
            fetch(group, i, buf, got).start()

        def put(group, i, buf, there):
            return pltpu.make_async_copy(buf.at[1], there.at[i], ssem.at[3 + group])

        def own_slice(group, i, buf, got, keep, out, compute):
            fetch(group, i, buf, got).wait()
            compute(2 * i + parity, buf.at[1], True)

            @pl.when(i == here)
            def _():
                put(group, i, buf, out).start()

            @pl.when(i != here)
            def _():
                put(group, i, buf, keep).start()

        def pass_slice(group, i, buf, keep, out):
            put(group, i, buf, keep).wait()

            @pl.when(i != here)
            def _():
                pltpu.make_async_remote_copy(
                    src_ref=keep.at[i], dst_ref=out.at[here], send_sem=sb.at[group * half + i],
                    recv_sem=rb.at[group * half + here], device_id=(2 * i + parity, t), device_id_type=MESH).start()

        def turn_of(i):
            return lax.rem(here + 1 + i, half)

        def first_grads(n2_v, sd, su, gsem):
            load_n2 = pltpu.make_async_copy(n2_h, n2_v, gsem)
            load_n2.start()
            rows_of, columns_of = by_rows(cot_v), by_columns(n2_v, dh_v)

            @pl.loop(0, half + 1)
            def _(i):
                now, before = turn_of(i), turn_of(i + half - 1)

                @pl.when(i > 0)
                def _():
                    get_slice(0, before, sd, ad_h)

                @pl.when(i < half)
                def _():
                    mate_slice(0, now, sd, ad_h, rows_of, i > 0)

                @pl.when(i < PACED)
                def _():
                    tick(done + jnp.maximum(3 * i - 1, 0))

                @pl.when(i > 0)
                def _():
                    own_slice(0, before, sd, ad_h, bd_h, gd_h, rows_of)
                    get_slice(1, before, su, au_h)

                @pl.when(i == 0)
                def _():
                    load_n2.wait()

                @pl.when(i < half)
                def _():
                    mate_slice(1, now, su, au_h, columns_of, i > 0)

                @pl.when(i < PACED)
                def _():
                    tick(done + jnp.maximum(3 * i, 1))

                @pl.when(i > 0)
                def _():
                    pass_slice(0, before, sd, bd_h, gd_h)
                    own_slice(1, before, su, au_h, bu_h, gu_h, columns_of)

                    @pl.when(i <= PACED)
                    def _():
                        tick(done + jnp.minimum(3 * i + 1, 3 * PACED - 1))

                    pass_slice(1, before, su, bu_h, gu_h)

            give(0, 0, sd, ad_h).wait_send()
            give(1, 0, su, au_h).wait_send()

        pl.run_scoped(
            first_grads, pltpu.VMEM((rows, cols), LOW), pltpu.VMEM((2, ff + att, width), F32),
            pltpu.VMEM((2, width, ff), F32), pltpu.SemaphoreType.DMA,
        )
        done2 = done + 3 * PACED

        def back_phase(dk, dv):
            for h in range(heads):
                dk[...] = jnp.zeros_like(dk)
                dv[...] = jnp.zeros_like(dv)

                @pl.loop(0, steps)
                def _(r):
                    rds, kds = at_tile(r, BLOCK), seen(r)
                    query, keys, values = q_v[h, rds, :], k_v[h, kds, :], v_v[h, kds, :]
                    d_ctx = do_v[rds, h * HS : (h + 1) * HS]
                    scores = jnp.where(allowed(r), dot_nt(query, keys) * score_scale, MASKED_SCORE)
                    probs = jnp.exp(scores - lse_v[rds, h * 64 : h * 64 + 1])
                    dv[kds, :] += dot_nn(probs.astype(LOW).T, d_ctx)
                    d_probs = dot_nt(d_ctx, values)
                    inner = jnp.sum(probs * d_probs, axis=-1, keepdims=True)
                    d_scores = (probs * (d_probs - inner)).astype(LOW)
                    d_query = dot_nn(d_scores, keys) * score_scale
                    d_query = turn(d_query, turn_tables(rot_v[rds, :]), -1).astype(LOW)
                    dq_v[rds, pl.ds(3 * h * HS, HS)] = d_query
                    dk[kds, :] += dot_nn(d_scores.T, query) * score_scale
                    there = pl.ds(3 * h * HS, HS)
                    sv_v[S_QKV : S_QKV + 1, there] += jnp.sum(d_query.astype(F32), axis=0, keepdims=True)

                if h == 0:
                    tick(done2)

                @pl.loop(0, steps)
                def _(r):
                    rds = at_tile(r, BLOCK)
                    d_key = turn(dk[rds, :], turn_tables(rot_v[rds, :]), -1).astype(LOW)
                    d_value = dv[rds, :].astype(LOW)
                    for part, got in ((1, d_key), (2, d_value)):
                        there = pl.ds((3 * h + part) * HS, HS)
                        dq_v[rds, there] = got
                        sv_v[S_QKV : S_QKV + 1, there] += jnp.sum(got.astype(F32), axis=0, keepdims=True)

                if h == 0 or h == heads - 1:
                    tick(done2 + (1 if h == 0 else 2))

        pl.run_scoped(back_phase, pltpu.VMEM((rows, HS), F32), pltpu.VMEM((rows, HS), F32))
        done3 = done2 + 3

        def norm_phase(xs, pst, xhat, rstd, m1, m2, xsem):
            load_x(0, xs, xsem).start()

            @pl.loop(0, steps)
            def _(r):
                rds = at_tile(r, BLOCK)
                xcur = xs.at[lax.rem(r, 2)]
                load_x(r, xs, xsem).wait()

                @pl.when(r + 1 < steps)
                def _():
                    load_x(r + 1, xs, xsem).start()

                @pl.loop(0, BLOCK // SUB, unroll=2)
                def _(s):
                    sds = at_tile(s, SUB)
                    xf = xcur[sds, :].astype(F32)
                    centre = xf - jnp.mean(xf, axis=-1, keepdims=True)
                    inv = lax.rsqrt(jnp.mean(centre * centre, axis=-1, keepdims=True) + EPSILON)
                    xhat[sds, :] = centre * inv
                    rstd[sds, :] = jnp.broadcast_to(inv, (SUB, 128))

                m1[...] = jnp.zeros_like(m1)
                m2[...] = jnp.zeros_like(m2)

                @pl.when(r > 1)
                def _():
                    put_p(r - 1, 1, pst).wait()

                @pl.loop(0, dtile)
                def _(j):
                    jds = at_tile(j, TILE)
                    xh = xhat[:, jds]
                    second = dot_nt(dh_v[rds, :], up_v[jds, :])
                    sv_v[S_GAIN2 : S_GAIN2 + 1, jds] += jnp.sum(second * xh, axis=0, keepdims=True)
                    sv_v[S_BIAS2 : S_BIAS2 + 1, jds] += jnp.sum(second, axis=0, keepdims=True)
                    first = dot_nt(dq_v[rds, :], qkv_v[jds, :])
                    sv_v[S_GAIN1 : S_GAIN1 + 1, jds] += jnp.sum(first * xh, axis=0, keepdims=True)
                    sv_v[S_BIAS1 : S_BIAS1 + 1, jds] += jnp.sum(first, axis=0, keepdims=True)
                    cot_tile = cot_v[rds, jds].astype(F32)
                    sv_v[S_OUT : S_OUT + 1, jds] += jnp.sum(cot_tile, axis=0, keepdims=True)
                    scaled = second * vec[V_GAIN2 : V_GAIN2 + 1, jds] + first * vec[V_GAIN1 : V_GAIN1 + 1, jds]
                    pst[:, :, jds] = scaled.reshape(PER, CH, TILE)
                    with_xh = scaled * xh
                    for q in range(TILE // 128):
                        m1[...] += scaled[:, q * 128 : (q + 1) * 128]
                        m2[...] += with_xh[:, q * 128 : (q + 1) * 128]

                tick(done3 + 2 * r)

                @pl.loop(0, PER)
                def _(s):
                    sds = at_tile(s, CH)
                    mean1 = jnp.sum(m1[sds, :], axis=-1, keepdims=True) * (1.0 / cols)
                    mean2 = jnp.sum(m2[sds, :], axis=-1, keepdims=True) * (1.0 / cols)
                    grad = rstd[sds, 0:1] * (pst[s] - mean1 - xhat[sds, :] * mean2)
                    cot_rows = cot_v[pl.ds(pl.multiple_of(r * BLOCK + s * CH, CH), CH), :].astype(F32)
                    pst[s] = grad + add_here * cot_rows

                put_p(r, 1, pst).start()

                @pl.when(r == 0)
                def _():
                    put_p(r, 1, pst).wait()

                tick(done3 + 2 * r + 1)

            put_p(steps - 1, 1, pst).wait()

        pl.run_scoped(
            norm_phase,
            pltpu.VMEM((2, BLOCK, cols), LOW), pltpu.VMEM((PER, CH, cols), F32), pltpu.VMEM((BLOCK, cols), F32),
            pltpu.VMEM((BLOCK, 128), F32), pltpu.VMEM((BLOCK, 128), F32), pltpu.VMEM((BLOCK, 128), F32),
            pltpu.SemaphoreType.DMA((2,)),
        )
        done4 = done3 + 2 * steps

        sv_v[S_STATS : S_STATS + 1, :] += (
            jnp.sum(csq_v[...]) * vec[V_CTX : V_CTX + 1, :]
            + jnp.sum(sq_v[...]) * vec[V_ACT : V_ACT + 1, :]
            + vec[V_COUNT : V_COUNT + 1, :]
        )
        svd[d] = sv_v[...]

        @pl.loop(1, ndp)
        def _(k):
            give_dp(k).start()

        def last_grads(n1_v, sq, gsem):
            load_n1 = pltpu.make_async_copy(n1_h, n1_v, gsem)
            load_n1.start()
            load_n1.wait()
            columns_of = by_columns(n1_v, dq_v)

            @pl.loop(0, half + 1)
            def _(i):
                now, before = turn_of(i), turn_of(i + half - 1)

                @pl.when(i > 0)
                def _():
                    get_slice(2, before, sq, aq_h)

                @pl.when(i < half)
                def _():
                    mate_slice(2, now, sq, aq_h, columns_of, i > 0)

                @pl.when(i < PACED)
                def _():
                    tick(done4 + jnp.maximum(2 * i - 1, 0))

                @pl.when(i > 0)
                def _():
                    own_slice(2, before, sq, aq_h, bq_h, gq_h, columns_of)

                    @pl.when(i <= PACED)
                    def _():
                        tick(done4 + jnp.minimum(2 * i, 2 * PACED - 1))

                    pass_slice(2, before, sq, bq_h, gq_h)

            give(2, 0, sq, aq_h).wait_send()

        pl.run_scoped(
            last_grads, pltpu.VMEM((rows, cols), LOW), pltpu.VMEM((2, width, qw), F32), pltpu.SemaphoreType.DMA)

    def give_dp(k):
        return pltpu.make_async_remote_copy(
            src_ref=sv_v, dst_ref=svd.at[d], send_sem=ssv.at[k], recv_sem=rsv.at[d],
            device_id=(lax.rem(d + k, ndp), t), device_id_type=MESH)

    def get_dp(k):
        other = lax.rem(d + k, ndp)
        return pltpu.make_async_remote_copy(
            src_ref=sv_v, dst_ref=svd.at[other], send_sem=ssv.at[k], recv_sem=rsv.at[other],
            device_id=(other, t), device_id_type=MESH)

    pl.run_scoped(with_inputs, pltpu.VMEM((cols, ff), LOW), pltpu.VMEM((cols, qw), LOW))
    finished = 4 * (steps - 1) + 1 + 3 * PACED + 3 + 2 * steps + 2 * PACED
    before_last = chunks + LAG - 5

    @pl.loop(finished, before_last)
    def _(k):
        tick(k)

    @pl.loop(1, ndp)
    def _(k):
        get_dp(k).wait_recv()
        give_dp(k).wait_send()

    total = svd[0]
    for i in range(1, ndp):
        total = total + svd[i]
    sv_o[0] = total
    svz[t] = total

    def give_z(k):
        return pltpu.make_async_remote_copy(
            src_ref=sv_o.at[0], dst_ref=svz.at[t], send_sem=ssz.at[k], recv_sem=rsz.at[t],
            device_id=(d, lax.rem(t + k, 4)), device_id_type=MESH)

    def get_z(k):
        other = lax.rem(t + k, 4)
        return pltpu.make_async_remote_copy(
            src_ref=sv_o.at[0], dst_ref=svz.at[other], send_sem=ssz.at[k], recv_sem=rsz.at[other],
            device_id=(d, other), device_id_type=MESH)

    for k in range(1, 4):
        give_z(k).start()

    @pl.loop(before_last, chunks + LAG)
    def _(k):
        tick(k)

    for k in range(1, 4):
        get_z(k).wait_recv()
        give_z(k).wait_send()
    sv_o[1] = svz[0] + svz[1] + svz[2] + svz[3]

    @pl.when(mid)
    def _():
        @pl.loop(chunks - HELD, chunks)
        def _(k):
            send_sum(k).wait_send()

    store(chunks - 2).wait()
    store(chunks - 1).wait()

    @pl.loop(0, half)
    def _(i):
        @pl.when(i != here)
        def _():
            for group, keep, out in ((0, bd_h, gd_h), (1, bu_h, gu_h), (2, bq_h, gq_h)):
                sent = pltpu.make_async_remote_copy(
                    src_ref=keep.at[i], dst_ref=out.at[i], send_sem=sb.at[group * half + i],
                    recv_sem=rb.at[group * half + i], device_id=(2 * i + parity, t), device_id_type=MESH)
                sent.wait_send()
                sent.wait_recv()


def layer(ndp, vec, seg, x, cot, rot, up_w, down_w, dense_w, qkv_w):
    rows, cols = x.shape
    ff, att, qw = up_w.shape[1], dense_w.shape[0], qkv_w.shape[1]
    heads = att // HS
    width, half, steps, chunks = cols // ndp, ndp // 2, rows // BLOCK, 2 * rows // CH
    any_spec = pl.BlockSpec(memory_space=pl.ANY)
    vmem_spec = pl.BlockSpec(memory_space=pltpu.VMEM)
    sem = pltpu.SemaphoreType.DMA
    slices = [
        jax.ShapeDtypeStruct((half, ff + att, width), F32),
        jax.ShapeDtypeStruct((half, width, ff), F32),
        jax.ShapeDtypeStruct((half, width, qw), F32),
    ]
    return pl.pallas_call(
        functools.partial(layer_kernel, ndp),
        out_shape=[
            jax.ShapeDtypeStruct((chunks, CH, cols), LOW),
            jax.ShapeDtypeStruct((2, SV, cols), F32),
            *slices,
            jax.ShapeDtypeStruct((chunks, CH, cols), F32),
            jax.ShapeDtypeStruct((rows, cols), LOW),
            jax.ShapeDtypeStruct((rows, cols), LOW),
            *slices,
            *slices,
        ],
        in_specs=[vmem_spec, vmem_spec] + [any_spec] * 7,
        out_specs=[any_spec, vmem_spec] + [any_spec] * 12,
        scratch_shapes=[
            pltpu.VMEM((ff + att, rows), LOW), pltpu.VMEM((rows, cols), LOW), pltpu.VMEM((rows, ff), LOW),
            pltpu.VMEM((rows, qw), LOW), pltpu.VMEM((heads, rows, HS), LOW), pltpu.VMEM((heads, rows, HS), LOW),
            pltpu.VMEM((heads, rows, HS), LOW), pltpu.VMEM((rows, att), LOW), pltpu.VMEM((rows, 64 * heads), F32),
            pltpu.VMEM((rows, 128), F32), pltpu.VMEM((SV, cols), F32),
            pltpu.VMEM((8, TILE), F32), pltpu.VMEM((8, HS), F32),
            pltpu.VMEM((ndp, SV, cols), F32), pltpu.VMEM((4, SV, cols), F32),
            pltpu.VMEM((WINDOW, CH, cols), F32), pltpu.VMEM((WINDOW, CH, cols), F32),
            pltpu.VMEM((2, CH, cols), F32), pltpu.VMEM((2, CH, cols), LOW),
            sem((WINDOW,)), sem((WINDOW,)), sem((WINDOW,)), sem((WINDOW,)), sem((2,)), sem((2,)),
            sem((steps + 1,)), sem((2 * (ff // TILE) + 2,)), sem, sem((2,)),
            sem((ndp,)), sem((ndp,)), sem((4,)), sem((4,)),
            sem((3,)), sem((3 * half,)), sem((3 * half,)), sem((3 * half,)), sem((6,)),
        ],
        compiler_params=pltpu.CompilerParams(
            collective_id=0, has_side_effects=True, vmem_limit_bytes=VMEM_ASK),
        cost_estimate=pl.CostEstimate(flops=10**11, bytes_accessed=2 * 10**8, transcendentals=0),
        name="layer",
    )(vec, seg, x, cot, rot, up_w, down_w, dense_w, qkv_w)


def turn_table(length):
    frequency = np.float32(10000.0) ** (-(np.float32(2.0) * np.arange(ROT // 2, dtype=np.float32)) / np.float32(ROT))
    angles = np.arange(length, dtype=np.float32)[:, None] * frequency.astype(np.float32)[None, :]
    angles = np.concatenate([angles, angles], axis=1).astype(np.float32)
    return np.concatenate([np.cos(angles), np.sin(angles)], axis=1).astype(np.float32)


def on_device(
    ndp,
    inputs,
    cotangent,
    segments,
    subsets,
    ln1_gain,
    ln1_bias,
    qkv_weight,
    qkv_bias,
    dense_weight,
    dense_bias,
    ln2_gain,
    ln2_bias,
    up_weight,
    up_bias,
    down_weight,
    down_bias,
):
    rows_here, model = inputs.shape
    hidden_here = up_weight.shape[1]
    lane = jnp.arange(model)
    slot_of = 3 * subsets[0]

    def row(values):
        return values if values.shape[0] == model else jnp.pad(values, (0, model - values.shape[0]))

    count = jnp.where(lax.axis_index("tensor") == 0, float(LEN), 0.0)
    blank = jnp.zeros((model,), F32)
    vec = jnp.stack(
        [
            row(up_bias), ln1_gain, ln1_bias, ln2_gain, ln2_bias, dense_bias + down_bias, row(qkv_bias),
            (lane == slot_of).astype(F32), (lane == slot_of + 1).astype(F32), jnp.where(lane == slot_of + 2, count, 0.0),
        ]
        + [blank] * (VROWS - 10)
    )
    seg = segments.astype(F32)
    done = layer(
        ndp, vec, seg, inputs, cotangent, jnp.asarray(turn_table(LEN)), up_weight, down_weight, dense_weight, qkv_weight)
    sums, small, grads_d, grads_u, grads_q = done[:5]
    sums = sums.reshape(2, rows_here, model)
    stats_total = small[1, S_STATS, : 3 * SUBSETS].reshape(SUBSETS, 3)
    widths = jnp.array([HEADS * HS, FF], jnp.float32)
    subset_rms = jnp.sqrt(
        stats_total[:, :2] / (jnp.maximum(stats_total[:, 2:3], 1.0) * widths[None, :])
    )
    bias_out = small[0, S_OUT]
    return (
        sums[0],
        sums[1],
        small[1, S_GAIN1],
        small[1, S_BIAS1],
        jnp.sum(grads_q, axis=0),
        small[0, S_QKV, : qkv_bias.shape[0]],
        jnp.sum(grads_d[:, hidden_here:], axis=0),
        bias_out,
        small[1, S_GAIN2],
        small[1, S_BIAS2],
        jnp.sum(grads_u, axis=0),
        small[0, S_UP, :hidden_here],
        jnp.sum(grads_d[:, :hidden_here], axis=0),
        bias_out,
        subset_rms,
    )


def solution(mesh):
    placed = (
        P("dp", None),
        P("dp", None),
        P("dp", None),
        P("dp"),
        P(),
        P(),
        P(None, "tensor"),
        P("tensor"),
        P("tensor", None),
        P(),
        P(),
        P(),
        P(None, "tensor"),
        P("tensor"),
        P("tensor", None),
        P(),
    )
    return jax.shard_map(
        functools.partial(on_device, mesh.shape["dp"]),
        mesh=mesh,
        in_specs=placed,
        out_specs=(
            P("dp", None),
            P("dp", None),
            P(),
            P(),
            P("dp", "tensor"),
            P("tensor"),
            P("tensor", "dp"),
            P(),
            P(),
            P(),
            P("dp", "tensor"),
            P("tensor"),
            P("tensor", "dp"),
            P(),
            P(),
        ),
        check_vma=False,
    )
```

time: 842 us -> 460 us (0.55); the launches traced: 826 us -> 454 us
  waiting for transfers between devices: 435 us -> 0 us
  Pallas kernels: 0 us -> 418 us
  matrix products: 190 us -> 0 us
  blocking collectives: 92.4 us -> 0 us
  other arithmetic: 59.8 us -> 20.8 us
  local copies, waits for them, and re-layouts: 30.9 us -> 14.1 us
  between operations: 17.5 us -> 1.37 us
    psum x1 -> x0, waiting for transfers between devices: 435 us -> none  [on_device(): branches = lax.psum(branch_terms, 'tensor')]
    pallas_call x0 -> x1, Pallas kernels: none -> 418 us  [layer(): pl.pallas_call(functools.partial(layer_kernel, ndp), out_shape=[jax.Shape...]
    dot_general x24 -> x0, matrix products: 190 us -> none  [the longest x4 53 us: dot_rows(): lax.dot_general(left, right, (((0,), (0,)), ((), ())), preferred_element_...]
    psum x3 -> x0, blocking collectives: 92.4 us -> none  [the longest x1 48.7 us: on_device(): stats_total = lax.psum(stats_local, ('dp', 'tensor'))]
    reduce_sum x8 -> x4, other arithmetic: 29.7 us -> 18.5 us  [the longest x1 5.72 us: on_device(): jnp.sum(grads_u, axis=0)]
    convert_element_type x4 -> x2, other arithmetic: 10.1 us -> 1.3 us  [the longest x1 1.28 us: on_device(): seg = segments.astype(F32)]
  transfers between devices with their start and end apart: 5 -> 0, of which waited for: 1 -> 0; matrix products, arithmetic and copies ran while one was open for 9% -> 0% of each run, Pallas kernels for 0% -> 0%
where the time goes in v3:
time: 460 us; the launch traced here: 454 us
  Pallas kernels  418 us (91%)
  other arithmetic  20.8 us (5%)
  local copies, waits for them, and re-layouts  14.1 us (3%)
    pallas_call x1, Pallas kernels, layer(): pl.pallas_call(functools.partial(layer_kernel, ndp), out_shape=[jax.Shape...  418 us

profile of v3, /device:TPU:10, one launch (start us, length us, event | category | flops | bytes accessed | tf_op | source)
XLA Modules:
  0.0 454.4 jit_solution(18243685056712679765)
XLA Ops:
  1.3 1.3 convert_element_type.27.seg
  2.6 0.7 pad.4
  3.3 0.7 add.11
  4.1 2.2 stack.42.vec
  6.2 418.1 %layer.1 = (bf16[64,32,2048]{2,1,0:T(8,128)(2,1)}, f32[2,8,2048]{2,1,0:T(8,128)}, f32[4,2560,256]{2,1,0:T(8,128)}, f32[4,256,2048]{2,1,0:T(8,128)}, f32[4,256,15...) custom-call(f32[16,2048]{1,0:T(8,128)} %stack.42.vec, ...), custom_call_target="tpu_custom_call" | custom-call | flops 99999997952 | bytes 200000000 | tf_op jit(solution)/shard_map/layer/pallas_call | solution.py:784
  424.3 0.0 copy-start.1
  424.3 6.1 %fusion.2 = (bf16[32,32,2048]{2,1,0:T(8,128)(2,1)}, bf16[32,32,2048]{2,1,0:T(8,128)(2,1)}) fusion(bf16[64,32,2048]{2,1,0:T(8,128)(2,1)} %get-tuple-element.20), kind=kLoop, calls=%fused_computation.11 | loop fusion | bytes 16777216 | tf_op jit(solution)/shard_map/slice | solution.py:875
  430.5 0.7 slice_reduce_fusion.3
  431.2 1.4 slice_reduce_fusion.2
  432.6 1.7 fusion.3
  434.3 0.0 copy-start
  434.3 0.1 reshape_squeeze.3
  434.4 0.2 fusion
  434.5 0.0 copy-done.1
  434.6 0.1 fusion.1
  434.6 0.7 copy.34
  435.3 2.6 slice_reduce_fusion.1
  437.9 5.5 %slice_reduce_fusion = f32[2048,256]{1,0:T(8,128)} fusion(f32[4,2560,256]{2,1,0:T(8,128)} %get-tuple-element.23), kind=kLoop, calls=%fused_computation | loop fusion | flops 1572864 | bytes 10485760 | tf_op jit(solution)/shard_map/reduce_sum | solution.py:886
  443.4 4.7 %reduce_sum.36 = f32[256,1536]{1,0:T(8,128)} reduce(f32[4,256,1536]{2,1,0:T(8,128)} %get-tuple-element.22, f32[]{:T(128)} %constant.10.clone.1), dimensions={0}, to_apply=%region_0.1 | reduce | flops 1179648 | bytes 7864324 | tf_op jit(solution)/shard_map/reduce_sum | solution.py:878
  448.1 5.7 %reduce_sum.38 = f32[256,2048]{1,0:T(8,128)} reduce(f32[4,256,2048]{2,1,0:T(8,128)} %get-tuple-element.24, f32[]{:T(128)} %constant.10.clone.1), dimensions={0}, to_apply=%region_2.3 | reduce | flops 1572864 | bytes 10485764 | tf_op jit(solution)/shard_map/reduce_sum | solution.py:884
  453.8 0.0 copy-done
  453.8 0.6 copy.37
  (4 shorter events, 0.0 us)
Async XLA Ops:
  424.3 10.2 %copy-start.1 = (f32[2]{0:T(128)S(1)}, f32[2]{0:T(128)}, u32[]{:S(2)}) copy-start(f32[2]{0:T(128)} %constant.27.clone) | copy-start | bytes 28
  434.3 19.5 %copy-start = (f32[1,1,2048]{2,1,0:T(1,128)}, f32[1,1,2048]{2,1,0:T(1,128)S(1)}, u32[]{:S(2)}) copy-start(f32[1,1,2048]{2,1,0:T(1,128)S(1)} %get-tuple-element.60) | copy-start | bytes 24580

commit v4 on v3

--- a/solution.py
+++ b/solution.py
@@ -31,6 +31,7 @@
 PER = BLOCK // CH
 WINDOW = 8
 HELD = 4
+BACK = 2
 LAG = 5
 PACED = 4
 TILE = 512
@@ -75,9 +76,9 @@
 
 def layer_kernel(
     ndp,
-    vec, seg, x_h, cot_h, rot_h, up_h, down_h, dense_h, qkv_h,
-    o_h, sv_o, gd_h, gu_h, gq_h, p_h, n1_h, n2_h, ad_h, au_h, aq_h, bd_h, bu_h, bq_h,
-    a_t, cot_v, dh_v, dq_v, q_v, k_v, v_v, do_v, lse_v, rot_v, sv_v, sq_v, csq_v, svd, svz,
+    up_b, qkv_b, gain1, bias1, gain2, bias2, dense_b, down_b, seg_in, subset, x_h, cot_h, rot_h, up_h, down_h, dense_h, qkv_h,
+    o_h, sv_o, down_g, dense_g, up_g, qkv_g, gd_h, gu_h, gq_h, p_h, n1_h, n2_h, ad_h, au_h, aq_h, bd_h, bu_h, bq_h,
+    vec, seg, a_t, cot_v, dh_v, dq_v, q_v, k_v, v_v, do_v, lse_v, rot_v, sv_v, sq_v, csq_v, svd, svz,
     near_in, far_in, own, low,
     s1, r1, s2, r2, lp, lo, lsem, wsem, psem, nsem,
     ssv, rsv, ssz, rsz, sa, ra, sb, rb, ssem,
@@ -182,9 +183,9 @@
             def _():
                 load_own(k + 2).start()
 
-        @pl.when(mid & (k >= 1) & (k < chunks + 1))
+        @pl.when(mid & (k >= BACK) & (k < chunks + BACK))
         def _():
-            j = k - 1
+            j = k - BACK
             swap(j).wait()
             far_in[slot(j)] = near_in[slot(j)] + far_in[slot(j)]
             send_sum(j).start()
@@ -213,6 +214,19 @@
         query_seg = jnp.broadcast_to(seg[0:1, at_tile(r, BLOCK)], (8, BLOCK)).T[:, 0:1]
         return (query_seg == seg[0:1, seen(r)]) & (key_at <= query_at)
 
+    vec[...] = jnp.zeros_like(vec)
+    for at, ref in (
+        (V_UP, up_b), (V_QKV, qkv_b), (V_GAIN1, gain1), (V_BIAS1, bias1), (V_GAIN2, gain2), (V_BIAS2, bias2), (V_OUT, dense_b)
+    ):
+        vec[at : at + 1, pl.ds(0, ref.shape[1])] = ref[...]
+    vec[V_OUT : V_OUT + 1, :] += down_b[...]
+    seg[...] = seg_in[...].astype(F32)
+    lane = lax.broadcasted_iota(jnp.int32, (1, cols), 1)
+    first_stat = 3 * subset[0]
+    vec[V_CTX : V_CTX + 1, :] = jnp.where(lane == first_stat, 1.0, 0.0)
+    vec[V_ACT : V_ACT + 1, :] = jnp.where(lane == first_stat + 1, 1.0, 0.0)
+    count = jnp.where(t == 0, 1.0, 0.0).astype(F32) * rows
+    vec[V_COUNT : V_COUNT + 1, :] = jnp.where(lane == first_stat + 2, count, 0.0)
     sv_v[...] = jnp.zeros_like(sv_v)
     sq_v[...] = jnp.zeros_like(sq_v)
     csq_v[...] = jnp.zeros_like(csq_v)
@@ -233,17 +247,8 @@
             load_x(0, xs, xsem).start()
             load_qkv.start()
             load_rot.start()
-            load_cot(0).start()
-            load_dense.start()
-            for j in range(ntile):
-                load_up(j).start()
-            for j in range(ntile):
-                load_down(j).start()
-            for r in range(1, steps):
-                load_cot(r).start()
             k_v[...] = jnp.zeros_like(k_v)
             v_v[...] = jnp.zeros_like(v_v)
-            pl.semaphore_wait(bar, 3 + ndp - 1)
 
             def put_n(r):
                 return (
@@ -282,6 +287,11 @@
                 def _():
                     load_qkv.wait()
                     load_rot.wait()
+                    for j in range(ntile):
+                        load_up(j).start()
+                    load_cot(0).start()
+                    load_dense.start()
+                    pl.semaphore_wait(bar, 3 + ndp - 1)
 
                 tables = turn_tables(rot_v[rds, :])
                 for h in range(heads):
@@ -292,13 +302,10 @@
                             head = turn(head, tables, 1)
                         (q_v, k_v, v_v)[part][h, rds, :] = head.astype(LOW)
 
-                load_cot(r).wait()
-
                 @pl.when(r == 0)
                 def _():
-                    load_dense.wait()
-
-                do_v[rds, :] = dot_nt(cot_v[rds, :], dense_v[...]).astype(LOW)
+                    for j in range(ntile):
+                        load_down(j).start()
 
                 ok = allowed(r)
                 for h in range(heads):
@@ -340,6 +347,10 @@
 
                 @pl.when(r == 0)
                 def _():
+                    load_dense.wait()
+                    for k in range(1, steps):
+                        load_cot(k).start()
+
                     @pl.loop(0, ntile)
                     def _(j):
                         load_down(j).wait()
@@ -367,6 +378,9 @@
                 @pl.when(r > 0)
                 def _():
                     tick(4 * r - 1)
+
+                load_cot(r).wait()
+                do_v[rds, :] = dot_nt(cot_v[rds, :], dense_v[...]).astype(LOW)
 
                 @pl.loop(0, ntile)
                 def _(j):
@@ -467,7 +481,7 @@
                     recv_sem=rb.at[group * half + here], device_id=(2 * i + parity, t), device_id_type=MESH).start()
 
         def turn_of(i):
-            return lax.rem(here + 1 + i, half)
+            return lax.bitwise_xor(here, half - 1 - lax.rem(i, half))
 
         def first_grads(n2_v, sd, su, gsem):
             load_n2 = pltpu.make_async_copy(n2_h, n2_v, gsem)
@@ -569,8 +583,9 @@
         pl.run_scoped(back_phase, pltpu.VMEM((rows, HS), F32), pltpu.VMEM((rows, HS), F32))
         done3 = done2 + 3
 
-        def norm_phase(xs, pst, xhat, rstd, m1, m2, xsem):
+        def norm_phase(n1_v, nsem1, xs, pst, xhat, rstd, m1, m2, xsem):
             load_x(0, xs, xsem).start()
+            pltpu.make_async_copy(n1_h, n1_v, nsem1).start()
 
             @pl.loop(0, steps)
             def _(r):
@@ -638,29 +653,10 @@
 
             put_p(steps - 1, 1, pst).wait()
 
-        pl.run_scoped(
-            norm_phase,
-            pltpu.VMEM((2, BLOCK, cols), LOW), pltpu.VMEM((PER, CH, cols), F32), pltpu.VMEM((BLOCK, cols), F32),
-            pltpu.VMEM((BLOCK, 128), F32), pltpu.VMEM((BLOCK, 128), F32), pltpu.VMEM((BLOCK, 128), F32),
-            pltpu.SemaphoreType.DMA((2,)),
-        )
         done4 = done3 + 2 * steps
 
-        sv_v[S_STATS : S_STATS + 1, :] += (
-            jnp.sum(csq_v[...]) * vec[V_CTX : V_CTX + 1, :]
-            + jnp.sum(sq_v[...]) * vec[V_ACT : V_ACT + 1, :]
-            + vec[V_COUNT : V_COUNT + 1, :]
-        )
-        svd[d] = sv_v[...]
-
-        @pl.loop(1, ndp)
-        def _(k):
-            give_dp(k).start()
-
-        def last_grads(n1_v, sq, gsem):
-            load_n1 = pltpu.make_async_copy(n1_h, n1_v, gsem)
-            load_n1.start()
-            load_n1.wait()
+        def last_grads(n1_v, nsem1, sq):
+            pltpu.make_async_copy(n1_h, n1_v, nsem1).wait()
             columns_of = by_columns(n1_v, dq_v)
 
             @pl.loop(0, half + 1)
@@ -691,8 +687,29 @@
 
             give(2, 0, sq, aq_h).wait_send()
 
-        pl.run_scoped(
-            last_grads, pltpu.VMEM((rows, cols), LOW), pltpu.VMEM((2, width, qw), F32), pltpu.SemaphoreType.DMA)
+        def small_sums():
+            sv_v[S_STATS : S_STATS + 1, :] += (
+                jnp.sum(csq_v[...]) * vec[V_CTX : V_CTX + 1, :]
+                + jnp.sum(sq_v[...]) * vec[V_ACT : V_ACT + 1, :]
+                + vec[V_COUNT : V_COUNT + 1, :]
+            )
+            svd[d] = sv_v[...]
+
+            @pl.loop(1, ndp)
+            def _(k):
+                give_dp(k).start()
+
+        def with_n1(n1_v, nsem1):
+            pl.run_scoped(
+                functools.partial(norm_phase, n1_v, nsem1),
+                pltpu.VMEM((2, BLOCK, cols), LOW), pltpu.VMEM((PER, CH, cols), F32), pltpu.VMEM((BLOCK, cols), F32),
+                pltpu.VMEM((BLOCK, 128), F32), pltpu.VMEM((BLOCK, 128), F32), pltpu.VMEM((BLOCK, 128), F32),
+                pltpu.SemaphoreType.DMA((2,)),
+            )
+            small_sums()
+            pl.run_scoped(functools.partial(last_grads, n1_v, nsem1), pltpu.VMEM((2, width, qw), F32))
+
+        pl.run_scoped(with_n1, pltpu.VMEM((rows, cols), LOW), pltpu.SemaphoreType.DMA)
 
     def give_dp(k):
         return pltpu.make_async_remote_copy(
@@ -707,22 +724,12 @@
 
     pl.run_scoped(with_inputs, pltpu.VMEM((cols, ff), LOW), pltpu.VMEM((cols, qw), LOW))
     finished = 4 * (steps - 1) + 1 + 3 * PACED + 3 + 2 * steps + 2 * PACED
-    before_last = chunks + LAG - 5
+    tiles_down, tiles_up, tiles_qkv = (ff + att) // TILE, ff // TILE, qw // TILE
+    before_last = chunks - tiles_down - tiles_up - 5
 
     @pl.loop(finished, before_last)
     def _(k):
         tick(k)
-
-    @pl.loop(1, ndp)
-    def _(k):
-        get_dp(k).wait_recv()
-        give_dp(k).wait_send()
-
-    total = svd[0]
-    for i in range(1, ndp):
-        total = total + svd[i]
-    sv_o[0] = total
-    svz[t] = total
 
     def give_z(k):
         return pltpu.make_async_remote_copy(
@@ -735,10 +742,93 @@
             src_ref=sv_o.at[0], dst_ref=svz.at[other], send_sem=ssz.at[k], recv_sem=rsz.at[other],
             device_id=(d, other), device_id_type=MESH)
 
-    for k in range(1, 4):
-        give_z(k).start()
-
-    @pl.loop(before_last, chunks + LAG)
+    def small_totals():
+        @pl.loop(1, ndp)
+        def _(k):
+            get_dp(k).wait_recv()
+            give_dp(k).wait_send()
+
+        total = svd[0]
+        for i in range(1, ndp):
+            total = total + svd[i]
+        sv_o[0] = total
+        svz[t] = total
+        for k in range(1, 4):
+            give_z(k).start()
+
+    def landed(group, keep, out):
+        @pl.loop(0, half)
+        def _(i):
+            @pl.when(i != here)
+            def _():
+                sent = pltpu.make_async_remote_copy(
+                    src_ref=keep.at[i], dst_ref=out.at[i], send_sem=sb.at[group * half + i],
+                    recv_sem=rb.at[group * half + i], device_id=(2 * i + parity, t), device_id_type=MESH)
+                sent.wait_send()
+                sent.wait_recv()
+
+    def sum_phase(tall, tall_sum, wide, wide_sum, fsem, usem):
+        def tiles_d():
+            for j in range((ff + att) // TILE):
+                there = down_g.at[pl.ds(j * TILE, TILE)] if j < ff // TILE else dense_g.at[pl.ds(j * TILE - ff, TILE)]
+                yield gd_h.at[:, pl.ds(j * TILE, TILE)], there
+
+        def tiles_w(got, result):
+            for j in range(got.shape[2] // TILE):
+                yield got.at[:, :, pl.ds(j * TILE, TILE)], result.at[:, pl.ds(j * TILE, TILE)]
+
+        def add_up(pairs, parts, total):
+            pairs = list(pairs)
+
+            def get(j):
+                return pltpu.make_async_copy(pairs[j][0], parts.at[j % 2], fsem.at[j % 2])
+
+            def put_sum(j):
+                return pltpu.make_async_copy(total.at[j % 2], pairs[j][1], usem.at[j % 2])
+
+            get(0).start()
+            for j in range(len(pairs)):
+                if j + 1 < len(pairs):
+                    get(j + 1).start()
+                get(j).wait()
+                if j >= 2:
+                    put_sum(j - 2).wait()
+                acc = parts[j % 2, 0]
+                for i in range(1, half):
+                    acc = acc + parts[j % 2, i]
+                total[j % 2] = acc
+                put_sum(j).start()
+                yield
+            for j in range(max(len(pairs) - 2, 0), len(pairs)):
+                put_sum(j).wait()
+
+        at = before_last
+        for group, keep, out, work in (
+            (0, bd_h, gd_h, lambda: add_up(tiles_d(), tall, tall_sum)),
+            (1, bu_h, gu_h, lambda: add_up(tiles_w(gu_h, up_g), wide, wide_sum)),
+            (2, bq_h, gq_h, lambda: add_up(tiles_w(gq_h, qkv_g), wide, wide_sum)),
+        ):
+            if group == 2:
+                small_totals()
+
+                @pl.loop(at, chunks + BACK)
+                def _(k):
+                    tick(k)
+
+                at = chunks + BACK
+            landed(group, keep, out)
+            for _ in work():
+                tick(at)
+                at += 1
+
+    pl.run_scoped(
+        sum_phase,
+        pltpu.VMEM((2, half, TILE, width), F32), pltpu.VMEM((2, TILE, width), F32),
+        pltpu.VMEM((2, half, width, TILE), F32), pltpu.VMEM((2, width, TILE), F32),
+        pltpu.SemaphoreType.DMA((2,)), pltpu.SemaphoreType.DMA((2,)),
+    )
+
+    @pl.loop(chunks + BACK + tiles_qkv, chunks + LAG)
     def _(k):
         tick(k)
 
@@ -756,19 +846,8 @@
     store(chunks - 2).wait()
     store(chunks - 1).wait()
 
-    @pl.loop(0, half)
-    def _(i):
-        @pl.when(i != here)
-        def _():
-            for group, keep, out in ((0, bd_h, gd_h), (1, bu_h, gu_h), (2, bq_h, gq_h)):
-                sent = pltpu.make_async_remote_copy(
-                    src_ref=keep.at[i], dst_ref=out.at[i], send_sem=sb.at[group * half + i],
-                    recv_sem=rb.at[group * half + i], device_id=(2 * i + parity, t), device_id_type=MESH)
-                sent.wait_send()
-                sent.wait_recv()
-
-
-def layer(ndp, vec, seg, x, cot, rot, up_w, down_w, dense_w, qkv_w):
+
+def layer(ndp, vectors, segments, subsets, x, cot, rot, up_w, down_w, dense_w, qkv_w):
     rows, cols = x.shape
     ff, att, qw = up_w.shape[1], dense_w.shape[0], qkv_w.shape[1]
     heads = att // HS
@@ -786,6 +865,10 @@
         out_shape=[
             jax.ShapeDtypeStruct((chunks, CH, cols), LOW),
             jax.ShapeDtypeStruct((2, SV, cols), F32),
+            jax.ShapeDtypeStruct((ff, width), F32),
+            jax.ShapeDtypeStruct((att, width), F32),
+            jax.ShapeDtypeStruct((width, ff), F32),
+            jax.ShapeDtypeStruct((width, qw), F32),
             *slices,
             jax.ShapeDtypeStruct((chunks, CH, cols), F32),
             jax.ShapeDtypeStruct((rows, cols), LOW),
@@ -793,9 +876,10 @@
             *slices,
             *slices,
         ],
-        in_specs=[vmem_spec, vmem_spec] + [any_spec] * 7,
-        out_specs=[any_spec, vmem_spec] + [any_spec] * 12,
+        in_specs=[vmem_spec] * 9 + [pl.BlockSpec(memory_space=pltpu.SMEM)] + [any_spec] * 7,
+        out_specs=[any_spec, vmem_spec] + [any_spec] * 16,
         scratch_shapes=[
+            pltpu.VMEM((VROWS, cols), F32), pltpu.VMEM((1, rows), F32),
             pltpu.VMEM((ff + att, rows), LOW), pltpu.VMEM((rows, cols), LOW), pltpu.VMEM((rows, ff), LOW),
             pltpu.VMEM((rows, qw), LOW), pltpu.VMEM((heads, rows, HS), LOW), pltpu.VMEM((heads, rows, HS), LOW),
             pltpu.VMEM((heads, rows, HS), LOW), pltpu.VMEM((rows, att), LOW), pltpu.VMEM((rows, 64 * heads), F32),
@@ -813,7 +897,7 @@
             collective_id=0, has_side_effects=True, vmem_limit_bytes=VMEM_ASK),
         cost_estimate=pl.CostEstimate(flops=10**11, bytes_accessed=2 * 10**8, transcendentals=0),
         name="layer",
-    )(vec, seg, x, cot, rot, up_w, down_w, dense_w, qkv_w)
+    )(*vectors, segments, subsets, x, cot, rot, up_w, down_w, dense_w, qkv_w)
 
 
 def turn_table(length):
@@ -844,25 +928,13 @@
 ):
     rows_here, model = inputs.shape
     hidden_here = up_weight.shape[1]
-    lane = jnp.arange(model)
-    slot_of = 3 * subsets[0]
-
-    def row(values):
-        return values if values.shape[0] == model else jnp.pad(values, (0, model - values.shape[0]))
-
-    count = jnp.where(lax.axis_index("tensor") == 0, float(LEN), 0.0)
-    blank = jnp.zeros((model,), F32)
-    vec = jnp.stack(
-        [
-            row(up_bias), ln1_gain, ln1_bias, ln2_gain, ln2_bias, dense_bias + down_bias, row(qkv_bias),
-            (lane == slot_of).astype(F32), (lane == slot_of + 1).astype(F32), jnp.where(lane == slot_of + 2, count, 0.0),
-        ]
-        + [blank] * (VROWS - 10)
-    )
-    seg = segments.astype(F32)
-    done = layer(
-        ndp, vec, seg, inputs, cotangent, jnp.asarray(turn_table(LEN)), up_weight, down_weight, dense_weight, qkv_weight)
-    sums, small, grads_d, grads_u, grads_q = done[:5]
+    vectors = [
+        values.reshape(1, -1)
+        for values in (up_bias, qkv_bias, ln1_gain, ln1_bias, ln2_gain, ln2_bias, dense_bias, down_bias)
+    ]
+    sums, small, down_grad, dense_grad, up_grad, qkv_grad = layer(
+        ndp, vectors, segments, subsets, inputs, cotangent, jnp.asarray(turn_table(LEN)),
+        up_weight, down_weight, dense_weight, qkv_weight)[:6]
     sums = sums.reshape(2, rows_here, model)
     stats_total = small[1, S_STATS, : 3 * SUBSETS].reshape(SUBSETS, 3)
     widths = jnp.array([HEADS * HS, FF], jnp.float32)
@@ -875,15 +947,15 @@
         sums[1],
         small[1, S_GAIN1],
         small[1, S_BIAS1],
-        jnp.sum(grads_q, axis=0),
+        qkv_grad,
         small[0, S_QKV, : qkv_bias.shape[0]],
-        jnp.sum(grads_d[:, hidden_here:], axis=0),
+        dense_grad,
         bias_out,
         small[1, S_GAIN2],
         small[1, S_BIAS2],
-        jnp.sum(grads_u, axis=0),
+        up_grad,
         small[0, S_UP, :hidden_here],
-        jnp.sum(grads_d[:, :hidden_here], axis=0),
+        down_grad,
         bias_out,
         subset_rms,
     )

time: 460 us -> 431 us (0.937)
  other arithmetic: 20.8 us -> 0.26 us
  Pallas kernels: 418 us -> 404 us
  local copies, waits for them, and re-layouts: 14.1 us -> 20.7 us
    reduce_sum x4 -> x0, other arithmetic: 18.5 us -> none  [the longest x1 5.72 us: on_device(): jnp.sum(grads_u, axis=0)]
    pallas_call x1, Pallas kernels: 418 us -> 404 us  [layer(): pl.pallas_call(functools.partial(layer_kernel, ndp), out_shape=[jax.Shape...]
    unnamed x6 -> x14, local copies, waits for them, and re-layouts: 1.26 us -> 9.17 us
where the time goes in v4:
time: 431 us; the launch traced here: 427 us
  Pallas kernels  404 us (94%)
  local copies, waits for them, and re-layouts  20.7 us (5%)
    pallas_call x1, Pallas kernels, layer(): pl.pallas_call(functools.partial(layer_kernel, ndp), out_shape=[jax.Shape...  404 us
    unnamed x14, local copies, waits for them, and re-layouts  9.17 us

profile of v4, /device:TPU:10, one launch (start us, length us, event | category | flops | bytes accessed | tf_op | source)
XLA Modules:
  0.0 426.8 jit_solution(14821612564188758821)
XLA Ops:
  1.3 1.3 reshape.61.qkv_b
  2.6 404.5 %layer.1 = (bf16[64,32,2048]{2,1,0:T(8,128)(2,1)}, f32[2,8,2048]{2,1,0:T(8,128)}, f32[2048,256]{1,0:T(8,128)}, f32[512,256]{1,0:T(8,128)}, f32[256,2048]{1,0:T(8...) custom-call(f32[1,2048]{1,0:T(1,128)} %bitcast.24, ...), custom_call_target="tpu_custom_call" | custom-call | flops 99999997952 | bytes 200000000 | tf_op jit(solution)/shard_map/layer/pallas_call | solution.py:863
  407.1 0.0 copy-start.3
  407.1 0.0 copy-start.1
  407.1 6.2 %fusion.2 = (bf16[32,32,2048]{2,1,0:T(8,128)(2,1)}, bf16[32,32,2048]{2,1,0:T(8,128)(2,1)}) fusion(bf16[64,32,2048]{2,1,0:T(8,128)(2,1)} %get-tuple-element.21), kind=kLoop, calls=%fused_computation.6 | loop fusion | bytes 16777216 | tf_op jit(solution)/shard_map/slice | solution.py:947
  413.3 0.0 copy-start
  413.3 0.8 slice_reduce_fusion.1
  414.2 1.4 slice_reduce_fusion
  415.6 1.7 fusion.3
  417.3 0.0 copy-start.2
  417.3 0.1 reshape_squeeze.3
  417.3 0.2 fusion
  417.5 0.0 copy-done.3
  417.5 0.1 fusion.1
  417.6 0.7 copy.34
  418.3 0.6 copy.41
  418.9 2.7 copy.42
  421.5 0.0 copy-done.1
  421.5 0.8 copy.43
  422.3 3.1 copy.44
  425.5 0.0 copy-done
  425.5 1.3 copy.45
  426.8 0.0 copy-done.2
Async XLA Ops:
  407.1 10.4 %copy-start.3 = (f32[2]{0:T(128)S(1)}, f32[2]{0:T(128)}, u32[]{:S(2)}) copy-start(f32[2]{0:T(128)} %constant.7.clone) | copy-start | bytes 28
  407.1 14.4 %copy-start.1 = (f32[512,256]{1,0:T(8,128)S(1)}, f32[512,256]{1,0:T(8,128)}, u32[]{:S(2)}) copy-start(f32[512,256]{1,0:T(8,128)} %get-tuple-element.116) | copy-start | bytes 1572868
  413.3 12.2 %copy-start = (f32[2048,256]{1,0:T(8,128)S(1)}, f32[2048,256]{1,0:T(8,128)}, u32[]{:S(2)}) copy-start(f32[2048,256]{1,0:T(8,128)} %get-tuple-element.122) | copy-start | bytes 6291460
  417.3 9.5 %copy-start.2 = (f32[1,1,2048]{2,1,0:T(1,128)}, f32[1,1,2048]{2,1,0:T(1,128)S(1)}, u32[]{:S(2)}) copy-start(f32[1,1,2048]{2,1,0:T(1,128)S(1)} %get-tuple-element.62) | copy-start | bytes 24580

commit v5 on v4

--- a/solution.py
+++ b/solution.py
@@ -218,7 +218,7 @@
     for at, ref in (
         (V_UP, up_b), (V_QKV, qkv_b), (V_GAIN1, gain1), (V_BIAS1, bias1), (V_GAIN2, gain2), (V_BIAS2, bias2), (V_OUT, dense_b)
     ):
-        vec[at : at + 1, pl.ds(0, ref.shape[1])] = ref[...]
+        vec[at : at + 1, pl.ds(0, ref.shape[-1])] = ref[...].reshape(1, ref.shape[-1])
     vec[V_OUT : V_OUT + 1, :] += down_b[...]
     seg[...] = seg_in[...].astype(F32)
     lane = lax.broadcasted_iota(jnp.int32, (1, cols), 1)
@@ -900,6 +900,79 @@
     )(*vectors, segments, subsets, x, cot, rot, up_w, down_w, dense_w, qkv_w)
 
 
+def flat_shape(size):
+    return (1, size) if size % 1024 == 0 else (size,)
+
+
+SMALL_ROWS = ((1, S_GAIN1), (1, S_BIAS1), (0, S_QKV), (0, S_OUT), (1, S_GAIN2), (1, S_BIAS2), (0, S_UP), (0, S_OUT))
+
+
+def finish_kernel(o_h, down_h, dense_h, up_h, qkv_h, small, *rest):
+    out, grad, down_g, dense_g, up_g, qkv_g = rest[:6]
+    row_refs, rms, held, sems_in, sems_out = rest[6:14], rest[14], rest[15:21], rest[21], rest[22]
+    half_chunks = out.shape[0]
+    copies = []
+    for index, (source, target) in enumerate((
+        (o_h.at[pl.ds(0, half_chunks)], out), (o_h.at[pl.ds(half_chunks, half_chunks)], grad),
+        (down_h, down_g), (dense_h, dense_g), (up_h, up_g), (qkv_h, qkv_g),
+    )):
+        count = source.shape[0] // PIECES
+        for piece in range(PIECES):
+            at = pl.ds(piece * count, count)
+            buf, sem = held[index].at[at], PIECES * index + piece
+            copies.append((
+                pltpu.make_async_copy(source.at[at], buf, sems_in.at[sem]),
+                pltpu.make_async_copy(buf, target.at[at], sems_out.at[sem]),
+            ))
+    for load, _ in copies:
+        load.start()
+    for (which, row), ref in zip(SMALL_ROWS, row_refs):
+        if len(ref.shape) == 1:
+            ref[...] = small[which, row, pl.ds(0, ref.shape[0])]
+        else:
+            ref[...] = small[which, row : row + 1, pl.ds(0, ref.shape[1])]
+    lane = lax.broadcasted_iota(jnp.int32, (128, 128), 1)
+    place = lax.broadcasted_iota(jnp.int32, (128, 128), 0)
+    stats = jnp.broadcast_to(small[1, S_STATS : S_STATS + 1, :128], (8, 128)).T[:, 0:1]
+    context, active, count = (
+        jnp.sum(jnp.where(place == 3 * lane + part, stats, 0.0), axis=0, keepdims=True) for part in range(3)
+    )
+    count = jnp.maximum(count, 1.0)
+    rms[0:1, :] = jnp.sqrt(context / (count * (HEADS * HS)))[:, :SUBSETS]
+    rms[1:2, :] = jnp.sqrt(active / (count * FF))[:, :SUBSETS]
+    for load, save in copies:
+        load.wait()
+        save.start()
+    for _, save in copies:
+        save.wait()
+
+
+PIECES = 4
+
+
+def finish(sums, small, down_grad, dense_grad, up_grad, qkv_grad):
+    chunks, per, cols = sums.shape
+    grads = (down_grad, dense_grad, up_grad, qkv_grad)
+    qw, ff = qkv_grad.shape[1], up_grad.shape[1]
+    any_spec = pl.BlockSpec(memory_space=pl.ANY)
+    vmem_spec = pl.BlockSpec(memory_space=pltpu.VMEM)
+    row_widths = [cols, cols, qw, cols, cols, cols, ff, cols]
+    return pl.pallas_call(
+        finish_kernel,
+        out_shape=[jax.ShapeDtypeStruct((chunks // 2, per, cols), LOW)] * 2
+        + [jax.ShapeDtypeStruct(grad.shape, F32) for grad in grads]
+        + [jax.ShapeDtypeStruct(flat_shape(row_width), F32) for row_width in row_widths]
+        + [jax.ShapeDtypeStruct((2, SUBSETS), F32)],
+        in_specs=[any_spec] * 5 + [vmem_spec],
+        out_specs=[any_spec] * 6 + [vmem_spec] * 9,
+        scratch_shapes=[pltpu.VMEM((chunks // 2, per, cols), LOW)] * 2
+        + [pltpu.VMEM(grad.shape, F32) for grad in grads]
+        + [pltpu.SemaphoreType.DMA((6 * PIECES,))] * 2,
+        compiler_params=pltpu.CompilerParams(vmem_limit_bytes=VMEM_ASK),
+        name="finish",
+    )(sums, *grads, small)
+
+
 def turn_table(length):
     frequency = np.float32(10000.0) ** (-(np.float32(2.0) * np.arange(ROT // 2, dtype=np.float32)) / np.float32(ROT))
     angles = np.arange(length, dtype=np.float32)[:, None] * frequency.astype(np.float32)[None, :]
@@ -927,37 +1000,34 @@
     down_bias,
 ):
     rows_here, model = inputs.shape
-    hidden_here = up_weight.shape[1]
     vectors = [
-        values.reshape(1, -1)
+        values.reshape(flat_shape(values.shape[0]))
         for values in (up_bias, qkv_bias, ln1_gain, ln1_bias, ln2_gain, ln2_bias, dense_bias, down_bias)
     ]
-    sums, small, down_grad, dense_grad, up_grad, qkv_grad = layer(
+    held = layer(
         ndp, vectors, segments, subsets, inputs, cotangent, jnp.asarray(turn_table(LEN)),
         up_weight, down_weight, dense_weight, qkv_weight)[:6]
-    sums = sums.reshape(2, rows_here, model)
-    stats_total = small[1, S_STATS, : 3 * SUBSETS].reshape(SUBSETS, 3)
-    widths = jnp.array([HEADS * HS, FF], jnp.float32)
-    subset_rms = jnp.sqrt(
-        stats_total[:, :2] / (jnp.maximum(stats_total[:, 2:3], 1.0) * widths[None, :])
+    done = finish(*held)
+    out, input_grad, down_grad, dense_grad, up_grad, qkv_grad = done[:6]
+    gain1, bias1, qkv_bias_grad, bias_out, gain2, bias2, up_bias_grad, bias_out_again = (
+        row.reshape(-1) for row in done[6:14]
     )
-    bias_out = small[0, S_OUT]
     return (
-        sums[0],
-        sums[1],
-        small[1, S_GAIN1],
-        small[1, S_BIAS1],
+        out.reshape(rows_here, model),
+        input_grad.reshape(rows_here, model),
+        gain1,
+        bias1,
         qkv_grad,
-        small[0, S_QKV, : qkv_bias.shape[0]],
+        qkv_bias_grad,
         dense_grad,
         bias_out,
-        small[1, S_GAIN2],
-        small[1, S_BIAS2],
+        gain2,
+        bias2,
         up_grad,
-        small[0, S_UP, :hidden_here],
+        up_bias_grad,
         down_grad,
-        bias_out,
-        subset_rms,
+        bias_out_again,
+        done[14].T,
     )
 
 

time: 431 us -> 422 us (0.979)
  local copies, waits for them, and re-layouts: 20.7 us -> 0 us
  Pallas kernels: 404 us -> 417 us
    pallas_call x0 -> x1, Pallas kernels: none -> 12.3 us  [finish(): pl.pallas_call(finish_kernel, out_shape=[jax.ShapeDtypeStruct((chunks //...]
    slice x4 -> x0, local copies, waits for them, and re-layouts: 10.1 us -> none  [the longest x1 6.2 us: on_device(): sums[1]]
    unnamed x14 -> x0, local copies, waits for them, and re-layouts: 9.17 us -> none
where the time goes in v5:
time: 422 us; the launch traced here: 418 us
  Pallas kernels  417 us (99%)
    pallas_call x1, Pallas kernels, layer(): pl.pallas_call(functools.partial(layer_kernel, ndp), out_shape=[jax.Shape...  405 us
    pallas_call x1, Pallas kernels, finish(): pl.pallas_call(finish_kernel, out_shape=[jax.ShapeDtypeStruct((chunks //...  12.3 us

profile of v5, /device:TPU:10, one launch (start us, length us, event | category | flops | bytes accessed | tf_op | source)
XLA Modules:
  0.0 418.3 jit_solution(3502773381797910542)
XLA Ops:
  1.3 404.5 %layer.1 = (bf16[64,32,2048]{2,1,0:T(8,128)(2,1)}, f32[2,8,2048]{2,1,0:T(8,128)}, f32[2048,256]{1,0:T(8,128)}, f32[512,256]{1,0:T(8,128)}, f32[256,2048]{1,0:T(8...) custom-call(f32[1,2048]{1,0:T(1,128)} %bitcast.19, ...), custom_call_target="tpu_custom_call" | custom-call | flops 99999997952 | bytes 200000000 | tf_op jit(solution)/shard_map/layer/pallas_call | solution.py:863
  405.8 12.3 %finish.1 = (bf16[32,32,2048]{2,1,0:T(8,128)(2,1)}, bf16[32,32,2048]{2,1,0:T(8,128)(2,1)}, f32[2048,256]{1,0:T(8,128)}, f32[512,256]{1,0:T(8,128)}, f32[256,2048...) custom-call(bf16[64,32,2048]{2,1,0:T(8,128)(2,1)} %get-tuple-element, ...), custom_call_target="tpu_custom_call" | custom-call | tf_op jit(solution)/shard_map/finish/pallas_call | solution.py:960

commit v6 on v5

--- a/solution.py
+++ b/solution.py
@@ -262,6 +262,11 @@
                 xcur = xs.at[lax.rem(r, 2)]
                 load_x(r, xs, xsem).wait()
 
+                @pl.when(r == 0)
+                def _():
+                    for j in range(ntile):
+                        load_up(j).start()
+
                 @pl.when(r + 1 < steps)
                 def _():
                     load_x(r + 1, xs, xsem).start()
@@ -287,10 +292,10 @@
                 def _():
                     load_qkv.wait()
                     load_rot.wait()
+                    load_dense.start()
                     for j in range(ntile):
-                        load_up(j).start()
+                        load_down(j).start()
                     load_cot(0).start()
-                    load_dense.start()
                     pl.semaphore_wait(bar, 3 + ndp - 1)
 
                 tables = turn_tables(rot_v[rds, :])
@@ -301,11 +306,6 @@
                         if part < 2:
                             head = turn(head, tables, 1)
                         (q_v, k_v, v_v)[part][h, rds, :] = head.astype(LOW)
-
-                @pl.when(r == 0)
-                def _():
-                    for j in range(ntile):
-                        load_down(j).start()
 
                 ok = allowed(r)
                 for h in range(heads):
@@ -924,7 +924,7 @@
                 pltpu.make_async_copy(source.at[at], buf, sems_in.at[sem]),
                 pltpu.make_async_copy(buf, target.at[at], sems_out.at[sem]),
             ))
-    for load, _ in copies:
+    for load, _ in copies[:DEPTH]:
         load.start()
     for (which, row), ref in zip(SMALL_ROWS, row_refs):
         if len(ref.shape) == 1:
@@ -940,14 +940,17 @@
     count = jnp.maximum(count, 1.0)
     rms[0:1, :] = jnp.sqrt(context / (count * (HEADS * HS)))[:, :SUBSETS]
     rms[1:2, :] = jnp.sqrt(active / (count * FF))[:, :SUBSETS]
-    for load, save in copies:
+    for index, (load, save) in enumerate(copies):
         load.wait()
         save.start()
+        if index + DEPTH < len(copies):
+            copies[index + DEPTH][0].start()
     for _, save in copies:
         save.wait()
 
 
 PIECES = 4
+DEPTH = 8
 
 
 def finish(sums, small, down_grad, dense_grad, up_grad, qkv_grad):

time: 422 us -> 422 us (level)
  no operation moved by 1% of the time
where the time goes in v6:
time: 422 us; the launch traced here: 418 us
  Pallas kernels  416 us (99%)
    pallas_call x1, Pallas kernels, layer(): pl.pallas_call(functools.partial(layer_kernel, ndp), out_shape=[jax.Shape...  404 us
    pallas_call x1, Pallas kernels, finish(): pl.pallas_call(finish_kernel, out_shape=[jax.ShapeDtypeStruct((chunks //...  12.5 us

profile of v6, /device:TPU:10, one launch (start us, length us, event | category | flops | bytes accessed | tf_op | source)
XLA Modules:
  0.0 417.5 jit_solution(10731830352391719253)
XLA Ops:
  1.3 403.6 %layer.1 = (bf16[64,32,2048]{2,1,0:T(8,128)(2,1)}, f32[2,8,2048]{2,1,0:T(8,128)}, f32[2048,256]{1,0:T(8,128)}, f32[512,256]{1,0:T(8,128)}, f32[256,2048]{1,0:T(8...) custom-call(f32[1,2048]{1,0:T(1,128)} %bitcast.19, ...), custom_call_target="tpu_custom_call" | custom-call | flops 99999997952 | bytes 200000000 | tf_op jit(solution)/shard_map/layer/pallas_call | solution.py:863
  404.9 12.5 %finish.1 = (bf16[32,32,2048]{2,1,0:T(8,128)(2,1)}, bf16[32,32,2048]{2,1,0:T(8,128)(2,1)}, f32[2048,256]{1,0:T(8,128)}, f32[512,256]{1,0:T(8,128)}, f32[256,2048...) custom-call(bf16[64,32,2048]{2,1,0:T(8,128)(2,1)} %get-tuple-element, ...), custom_call_target="tpu_custom_call" | custom-call | tf_op jit(solution)/shard_map/finish/pallas_call | solution.py:963
